TPU v7x, 32 devices: a whole 2x2x4 slice. The times are simulated.
32 devices in a mesh: dom: 4 (over y, core), blk: 8 (over z, x).
Axes of the slice: x: 2, y: 2, z: 4, core: 2. Of those that a mesh axis runs over, the one named last changes fastest.
Arguments:
- particles: bfloat16 [1024, 9216], P(('dom', 'blk')), may hold values from -6 to 6
- references: bfloat16 [32, 9216], P('blk'), may hold values from -0.3 to 0.3
- inv_noise: float32 [1024], P(('dom', 'blk')), may hold values from 0.25 to 2
- significant: int32 [1024, 8], P(('dom', 'blk')), may hold values from 0 to 31, as said below
- sig_count: int32 [1024], P(('dom', 'blk')), may hold values from 2 to 8
Outputs:
- class_sums: float32 [32, 9216], P('blk', 'dom')
- class_weights: float32 [32], P('blk')
- log_evidence: float32 [1024], P(('dom', 'blk'))
Inputs may be any that keep to these rules, and one draw needn't show every extreme that they name: `significant`: each row holds 8 class ids with distinct values of id // 4; in the rows of one device, at most 32 slots (used or not) name classes with the same id // 4, and some value is named exactly 32 times.
All inputs are finite; a program needn't handle non-finite values.
Results may differ from a plain program's by a relative error of at most 0.0025.
Values may be sent and summed in bfloat16 or wider, within the bound.
No kernel may reach another device: no remote copies, remote signals or barrier semaphores. Data moves between devices by JAX's collectives and lax.ppermute only.
A program may use at most 64 MiB of HBM per device.

v0:
```python
import jax
import jax.numpy as jnp
from jax import lax
from jax.sharding import PartitionSpec as P

ROTS = 36


def shifted(block, axis, distance):
    devices = range(lax.axis_size(axis))
    route = [((i - distance) % len(devices), i) for i in devices]
    return lax.ppermute(block, axis, route)


def lag_table(rot_count):
    position = jnp.arange(rot_count * rot_count, dtype=jnp.int32)
    lag = (position // rot_count - position % rot_count) % rot_count
    return (lag[:, None] == jnp.arange(rot_count, dtype=jnp.int32)[None, :]).astype(jnp.float32)


def correlate(shaped, ref_block, inverse, table):
    class_width = ref_block.shape[0]
    ref_shaped = ref_block.reshape(class_width, shaped.shape[1], shaped.shape[2])
    pairs = jnp.einsum("iqj,kpj->ikqp", shaped, ref_shaped, preferred_element_type=jnp.float32)
    flat = pairs.reshape(shaped.shape[0] * class_width, -1)
    corr = jnp.dot(flat, table, precision=lax.Precision.HIGHEST).reshape(
        shaped.shape[0], class_width, -1
    )
    ref_wide = ref_block.astype(jnp.float32)
    norms = jnp.sum(ref_wide * ref_wide, axis=1)
    return inverse[:, None, None] * (corr - 0.5 * norms[None, :, None])


def contribute(weights_block, shaped, spread):
    particle_count, class_width, rot_count = weights_block.shape
    mixed = jnp.dot(
        weights_block.reshape(particle_count * class_width, rot_count),
        spread,
        preferred_element_type=jnp.float32,
    ).astype(jnp.bfloat16)
    mixed = mixed.reshape(particle_count, class_width, rot_count, rot_count)
    summed = jnp.einsum("ikqp,iqj->kpj", mixed, shaped, preferred_element_type=jnp.float32)
    return summed.reshape(class_width, rot_count * shaped.shape[2])


def body(particles, references, inv_noise, significant, sig_count):
    cycle_size = lax.axis_size("blk")
    my_index = lax.axis_index("blk")
    particle_count, pixel_count = particles.shape
    class_width = references.shape[0]
    slot_total = significant.shape[1]
    shaped = particles.reshape(particle_count, ROTS, pixel_count // ROTS)
    table = lag_table(ROTS)
    spread = table.T.astype(jnp.bfloat16)
    score_store = jnp.zeros((particle_count, cycle_size, class_width, ROTS), jnp.float32)

    def place(store_now, ref_block, anchor):
        update = correlate(shaped, ref_block, inv_noise, table)[:, None]
        return lax.dynamic_update_slice_in_dim(store_now, update, anchor, 1)

    score_store = place(score_store, references, my_index)

    def advance(turn_index, loop_state):
        ref_block, store_now = loop_state
        ref_block = shifted(ref_block, "blk", 1)
        return (ref_block, place(store_now, ref_block, (my_index - turn_index) % cycle_size))

    final_block, score_store = lax.fori_loop(1, cycle_size, advance, (references, score_store))
    scores = score_store.reshape(particle_count, cycle_size * class_width, ROTS)
    classes = jnp.arange(cycle_size * class_width, dtype=jnp.int32)
    slot_index = jnp.arange(slot_total, dtype=jnp.int32)
    live_slot = slot_index[None, :] < sig_count[:, None]
    matches = (significant[:, :, None] == classes[None, None, :]) & live_slot[:, :, None]
    class_mask = jnp.any(matches, axis=1)
    masked = jnp.where(class_mask[:, :, None], scores, -jnp.inf)
    row_peak = jnp.max(masked, axis=(1, 2))
    exp_terms = jnp.where(class_mask[:, :, None], jnp.exp(masked - row_peak[:, None, None]), 0.0)
    row_total = jnp.sum(exp_terms, axis=(1, 2))
    posterior = exp_terms / row_total[:, None, None]
    log_evidence = row_peak + jnp.log(row_total)
    totals = lax.psum(jnp.sum(posterior, axis=(0, 2)), ("dom", "blk"))
    class_weights = lax.dynamic_slice_in_dim(totals, my_index * class_width, class_width)
    weights_bf = posterior.astype(jnp.bfloat16).reshape(
        particle_count, cycle_size, class_width, ROTS
    )

    def pick(block_index):
        return lax.dynamic_index_in_dim(weights_bf, block_index, 1, keepdims=False)

    def gather_block(turn_index, partial_sum):
        partial_sum = shifted(partial_sum, "blk", 1)
        return partial_sum + contribute(
            pick((my_index - 1 - turn_index) % cycle_size), shaped, spread
        )

    start_sum = contribute(pick((my_index - 1) % cycle_size), shaped, spread)
    partial_value = lax.fori_loop(1, cycle_size, gather_block, start_sum)
    class_sums = lax.psum_scatter(partial_value, "dom", scatter_dimension=1, tiled=True)
    return (class_sums, class_weights, log_evidence)


def solution(mesh):
    in_specs = (
        P(("dom", "blk"), None),
        P("blk", None),
        P(("dom", "blk")),
        P(("dom", "blk"), None),
        P(("dom", "blk")),
    )
    out_specs = (P("blk", "dom"), P("blk"), P(("dom", "blk")))
    return jax.shard_map(body, mesh=mesh, in_specs=in_specs, out_specs=out_specs, check_vma=False)
```

profile of v0, /device:TPU:0, one launch (start us, length us, event | category | flops | bytes accessed | tf_op | source)
XLA Modules:
  0.0 241.9 jit_solution(16366987058999260800)
XLA Ops:
  12.6 2.4 copy.42
  15.0 2.3 dot_general.52
  19.4 99.3 %while.34 = (s32[]{:T(128)}, bf16[4,9216]{1,0:T(4,128)(2,1)S(1)}, f32[32,8,4,36]{3,2,1,0:T(4,128)}, f32[32]{0:T(128)S(1)}, bf16[32,36,256]{2,1,0:T(8,128)(2,1)S(...) while((s32[]{:T(128)}, bf16[4,9216]{1,0:T(4,128)(2,1)S(1)}, ...), condition=%wide.region_4.5_spmd.clone, body=%wide.region_2.4_spmd.clone.sunk | while | flops 156811408 | bytes 5416500 | solution.py:68
  19.4 2.9 %collective-permute-start = (bf16[4,9216]{1,0:T(4,128)(2,1)S(1)}, bf16[4,9216]{1,0:T(4,128)(2,1)S(1)}, u32[]{:S(2)}, u32[]{:S(2)}) collective-permute-start(bf16[4,9216]{1,0:T(4,128)(2,1)S(1)} %get-tuple-element.522), channel_id=1, source_target_pairs={{7,0},{0,1},{1,2},{2,3},{3,4},{4,5},{5,6},{6,7},{15,8},{8,9},{9,10... | collective-permute-start | bytes 221192 | tf_op jit(solution)/shard_map/while/body/eval_jaxpr/ppermute | solution.py:12
  22.4 5.4 %collective-permute-done = bf16[4,9216]{1,0:T(4,128)(2,1)S(1)} collective-permute-done((bf16[4,9216]{1,0:T(4,128)(2,1)S(1)}, bf16[4,9216]{1,0:T(4,128)(2,1)S(1)}, u32[]{:S(2)}, u32[]{:S(2)}) %collective-permute-start) | collective-permute-done | bytes 73760 | tf_op jit(solution)/shard_map/while/body/eval_jaxpr/ppermute | solution.py:12
  28.3 2.4 copy.67
  30.7 2.3 dot_general.62
  34.7 7.0 %collective-permute-done = bf16[4,9216]{1,0:T(4,128)(2,1)S(1)} collective-permute-done((bf16[4,9216]{1,0:T(4,128)(2,1)S(1)}, bf16[4,9216]{1,0:T(4,128)(2,1)S(1)}, u32[]{:S(2)}, u32[]{:S(2)}) %collective-permute-start) | collective-permute-done | bytes 73760 | tf_op jit(solution)/shard_map/while/body/eval_jaxpr/ppermute | solution.py:12
  42.3 2.4 copy.67
  44.7 2.3 dot_general.62
  48.7 7.0 %collective-permute-done = bf16[4,9216]{1,0:T(4,128)(2,1)S(1)} collective-permute-done((bf16[4,9216]{1,0:T(4,128)(2,1)S(1)}, bf16[4,9216]{1,0:T(4,128)(2,1)S(1)}, u32[]{:S(2)}, u32[]{:S(2)}) %collective-permute-start) | collective-permute-done | bytes 73760 | tf_op jit(solution)/shard_map/while/body/eval_jaxpr/ppermute | solution.py:12
  56.3 2.4 copy.67
  58.7 2.3 dot_general.62
  62.7 7.0 %collective-permute-done = bf16[4,9216]{1,0:T(4,128)(2,1)S(1)} collective-permute-done((bf16[4,9216]{1,0:T(4,128)(2,1)S(1)}, bf16[4,9216]{1,0:T(4,128)(2,1)S(1)}, u32[]{:S(2)}, u32[]{:S(2)}) %collective-permute-start) | collective-permute-done | bytes 73760 | tf_op jit(solution)/shard_map/while/body/eval_jaxpr/ppermute | solution.py:12
  70.3 2.4 copy.67
  76.8 7.0 %collective-permute-done = bf16[4,9216]{1,0:T(4,128)(2,1)S(1)} collective-permute-done((bf16[4,9216]{1,0:T(4,128)(2,1)S(1)}, bf16[4,9216]{1,0:T(4,128)(2,1)S(1)}, u32[]{:S(2)}, u32[]{:S(2)}) %collective-permute-start) | collective-permute-done | bytes 73760 | tf_op jit(solution)/shard_map/while/body/eval_jaxpr/ppermute | solution.py:12
  84.4 2.4 copy.67
  90.8 7.0 %collective-permute-done = bf16[4,9216]{1,0:T(4,128)(2,1)S(1)} collective-permute-done((bf16[4,9216]{1,0:T(4,128)(2,1)S(1)}, bf16[4,9216]{1,0:T(4,128)(2,1)S(1)}, u32[]{:S(2)}, u32[]{:S(2)}) %collective-permute-start) | collective-permute-done | bytes 73760 | tf_op jit(solution)/shard_map/while/body/eval_jaxpr/ppermute | solution.py:12
  98.4 2.4 copy.67
  104.8 7.0 %collective-permute-done = bf16[4,9216]{1,0:T(4,128)(2,1)S(1)} collective-permute-done((bf16[4,9216]{1,0:T(4,128)(2,1)S(1)}, bf16[4,9216]{1,0:T(4,128)(2,1)S(1)}, u32[]{:S(2)}, u32[]{:S(2)}) %collective-permute-start) | collective-permute-done | bytes 73760 | tf_op jit(solution)/shard_map/while/body/eval_jaxpr/ppermute | solution.py:12
  112.4 2.4 copy.67
  126.0 57.4 %while.35 = (s32[]{:T(128)}, f32[4,9216]{1,0:T(4,128)S(1)}, s32[]{:T(128)}, bf16[32,8,4,36]{3,2,1,0:T(4,128)(2,1)}, bf16[32,36,256]{2,1,0:T(8,128)(2,1)S(1)}, /*...) while((s32[]{:T(128)}, f32[4,9216]{1,0:T(4,128)S(1)}, s32[]{:T(128)}, ...), condition=%wide.region_8.9_spmd.clone, body=%wide.region_7.8_spmd.clone.sunk | while | flops 97221328 | bytes 4088172 | solution.py:97
  129.0 4.9 %collective-permute-done.1 = f32[4,9216]{1,0:T(4,128)S(1)} collective-permute-done((f32[4,9216]{1,0:T(4,128)S(1)}, f32[4,9216]{1,0:T(4,128)S(1)}, u32[]{:S(2)}, u32[]{:S(2)}) %collective-permute-start.1) | collective-permute-done | bytes 147488 | tf_op jit(solution)/shard_map/while/body/eval_jaxpr/ppermute | solution.py:12
  137.0 4.9 %collective-permute-done.1 = f32[4,9216]{1,0:T(4,128)S(1)} collective-permute-done((f32[4,9216]{1,0:T(4,128)S(1)}, f32[4,9216]{1,0:T(4,128)S(1)}, u32[]{:S(2)}, u32[]{:S(2)}) %collective-permute-start.1) | collective-permute-done | bytes 147488 | tf_op jit(solution)/shard_map/while/body/eval_jaxpr/ppermute | solution.py:12
  144.9 4.9 %collective-permute-done.1 = f32[4,9216]{1,0:T(4,128)S(1)} collective-permute-done((f32[4,9216]{1,0:T(4,128)S(1)}, f32[4,9216]{1,0:T(4,128)S(1)}, u32[]{:S(2)}, u32[]{:S(2)}) %collective-permute-start.1) | collective-permute-done | bytes 147488 | tf_op jit(solution)/shard_map/while/body/eval_jaxpr/ppermute | solution.py:12
  152.9 5.2 %collective-permute-done.1 = f32[4,9216]{1,0:T(4,128)S(1)} collective-permute-done((f32[4,9216]{1,0:T(4,128)S(1)}, f32[4,9216]{1,0:T(4,128)S(1)}, u32[]{:S(2)}, u32[]{:S(2)}) %collective-permute-start.1) | collective-permute-done | bytes 147488 | tf_op jit(solution)/shard_map/while/body/eval_jaxpr/ppermute | solution.py:12
  161.1 6.3 %collective-permute-done.1 = f32[4,9216]{1,0:T(4,128)S(1)} collective-permute-done((f32[4,9216]{1,0:T(4,128)S(1)}, f32[4,9216]{1,0:T(4,128)S(1)}, u32[]{:S(2)}, u32[]{:S(2)}) %collective-permute-start.1) | collective-permute-done | bytes 147488 | tf_op jit(solution)/shard_map/while/body/eval_jaxpr/ppermute | solution.py:12
  170.5 4.9 %collective-permute-done.1 = f32[4,9216]{1,0:T(4,128)S(1)} collective-permute-done((f32[4,9216]{1,0:T(4,128)S(1)}, f32[4,9216]{1,0:T(4,128)S(1)}, u32[]{:S(2)}, u32[]{:S(2)}) %collective-permute-start.1) | collective-permute-done | bytes 147488 | tf_op jit(solution)/shard_map/while/body/eval_jaxpr/ppermute | solution.py:12
  178.5 4.9 %collective-permute-done.1 = f32[4,9216]{1,0:T(4,128)S(1)} collective-permute-done((f32[4,9216]{1,0:T(4,128)S(1)}, f32[4,9216]{1,0:T(4,128)S(1)}, u32[]{:S(2)}, u32[]{:S(2)}) %collective-permute-start.1) | collective-permute-done | bytes 147488 | tf_op jit(solution)/shard_map/while/body/eval_jaxpr/ppermute | solution.py:12
  183.4 2.9 %copy.54 = f32[4,9216]{0,1:T(8,128)} copy(f32[4,9216]{1,0:T(4,128)S(1)} %get-tuple-element.339) | data formatting | bytes 294912
  186.4 37.2 %psum.7 = f32[32]{0:T(128)S(1)} all-reduce(f32[32]{0:T(128)S(1)} %reduce_sum.48), channel_id=1, replica_groups=mesh['dom'=4,'blk'=8] {'dom','blk'}, use_global_device_ids=true, to_apply=%region_11.12 | all-reduce | flops 32 | bytes 256 | tf_op jit(solution)/shard_map/psum | solution.py:81
  224.6 8.1 %reduce-scatter.4.cloned.1.call-done = f32[2304,4]{1,0:T(8,128)} async-done(((f32[9216,4]{1,0:T(8,128)}), f32[2304,4]{1,0:T(8,128)}) %reduce-scatter.4.cloned.1.call-update) | async-done | bytes 36880
  (162 shorter events, 63.8 us)
Async XLA Ops:
  7.2 3.5 %copy-start.3 = (bf16[32,9216]{1,0:T(8,128)(2,1)S(1)}, bf16[32,9216]{1,0:T(8,128)(2,1)}, u32[]{:S(2)}) copy-start(bf16[32,9216]{1,0:T(8,128)(2,1)} %param.9) | copy-start | bytes 1769476
  7.2 225.6 %reduce-scatter.4.cloned.1.call-start = ((), (), s32[]{:S(2)}) async-start(), calls=%async_computation.1 | async-start | bytes 5898240
  15.0 2.3 copy-start.6
  15.0 2.4 %copy-start.7 = (s32[32]{0:T(128)S(1)}, s32[32]{0:T(128)}, u32[]{:S(2)}) copy-start(s32[32]{0:T(128)} %param.13) | copy-start | bytes 388
  15.0 2.9 %copy-start.5 = (f32[32]{0:T(128)S(1)}, f32[32]{0:T(128)}, u32[]{:S(2)}) copy-start(f32[32]{0:T(128)} %param.11) | copy-start | bytes 388
  18.6 0.8 copy-start
  19.4 8.3 %collective-permute-start = (bf16[4,9216]{1,0:T(4,128)(2,1)S(1)}, bf16[4,9216]{1,0:T(4,128)(2,1)S(1)}, u32[]{:S(2)}, u32[]{:S(2)}) collective-permute-start(bf16[4,9216]{1,0:T(4,128)(2,1)S(1)} %get-tuple-element.522), channel_id=1, source_target_pairs={{7,0},{0,1},{1,2},{2,3},{3,4},{4,5},{5,6},{6,7},{15,8},{8,9},{9,10... | collective-permute-start | bytes 221192 | tf_op jit(solution)/shard_map/while/body/eval_jaxpr/ppermute | solution.py:12
  34.6 7.1 %collective-permute-start = (bf16[4,9216]{1,0:T(4,128)(2,1)S(1)}, bf16[4,9216]{1,0:T(4,128)(2,1)S(1)}, u32[]{:S(2)}, u32[]{:S(2)}) collective-permute-start(bf16[4,9216]{1,0:T(4,128)(2,1)S(1)} %get-tuple-element.522), channel_id=1, source_target_pairs={{7,0},{0,1},{1,2},{2,3},{3,4},{4,5},{5,6},{6,7},{15,8},{8,9},{9,10... | collective-permute-start | bytes 221192 | tf_op jit(solution)/shard_map/while/body/eval_jaxpr/ppermute | solution.py:12
  48.7 7.1 %collective-permute-start = (bf16[4,9216]{1,0:T(4,128)(2,1)S(1)}, bf16[4,9216]{1,0:T(4,128)(2,1)S(1)}, u32[]{:S(2)}, u32[]{:S(2)}) collective-permute-start(bf16[4,9216]{1,0:T(4,128)(2,1)S(1)} %get-tuple-element.522), channel_id=1, source_target_pairs={{7,0},{0,1},{1,2},{2,3},{3,4},{4,5},{5,6},{6,7},{15,8},{8,9},{9,10... | collective-permute-start | bytes 221192 | tf_op jit(solution)/shard_map/while/body/eval_jaxpr/ppermute | solution.py:12
  62.7 7.1 %collective-permute-start = (bf16[4,9216]{1,0:T(4,128)(2,1)S(1)}, bf16[4,9216]{1,0:T(4,128)(2,1)S(1)}, u32[]{:S(2)}, u32[]{:S(2)}) collective-permute-start(bf16[4,9216]{1,0:T(4,128)(2,1)S(1)} %get-tuple-element.522), channel_id=1, source_target_pairs={{7,0},{0,1},{1,2},{2,3},{3,4},{4,5},{5,6},{6,7},{15,8},{8,9},{9,10... | collective-permute-start | bytes 221192 | tf_op jit(solution)/shard_map/while/body/eval_jaxpr/ppermute | solution.py:12
  76.7 7.1 %collective-permute-start = (bf16[4,9216]{1,0:T(4,128)(2,1)S(1)}, bf16[4,9216]{1,0:T(4,128)(2,1)S(1)}, u32[]{:S(2)}, u32[]{:S(2)}) collective-permute-start(bf16[4,9216]{1,0:T(4,128)(2,1)S(1)} %get-tuple-element.522), channel_id=1, source_target_pairs={{7,0},{0,1},{1,2},{2,3},{3,4},{4,5},{5,6},{6,7},{15,8},{8,9},{9,10... | collective-permute-start | bytes 221192 | tf_op jit(solution)/shard_map/while/body/eval_jaxpr/ppermute | solution.py:12
  90.7 7.1 %collective-permute-start = (bf16[4,9216]{1,0:T(4,128)(2,1)S(1)}, bf16[4,9216]{1,0:T(4,128)(2,1)S(1)}, u32[]{:S(2)}, u32[]{:S(2)}) collective-permute-start(bf16[4,9216]{1,0:T(4,128)(2,1)S(1)} %get-tuple-element.522), channel_id=1, source_target_pairs={{7,0},{0,1},{1,2},{2,3},{3,4},{4,5},{5,6},{6,7},{15,8},{8,9},{9,10... | collective-permute-start | bytes 221192 | tf_op jit(solution)/shard_map/while/body/eval_jaxpr/ppermute | solution.py:12
  104.7 7.1 %collective-permute-start = (bf16[4,9216]{1,0:T(4,128)(2,1)S(1)}, bf16[4,9216]{1,0:T(4,128)(2,1)S(1)}, u32[]{:S(2)}, u32[]{:S(2)}) collective-permute-start(bf16[4,9216]{1,0:T(4,128)(2,1)S(1)} %get-tuple-element.522), channel_id=1, source_target_pairs={{7,0},{0,1},{1,2},{2,3},{3,4},{4,5},{5,6},{6,7},{15,8},{8,9},{9,10... | collective-permute-start | bytes 221192 | tf_op jit(solution)/shard_map/while/body/eval_jaxpr/ppermute | solution.py:12
  118.7 3.6 %copy-start.1 = (f32[32,8,4,36]{3,2,1,0:T(4,128)S(1)}, f32[32,8,4,36]{3,2,1,0:T(4,128)}, u32[]{:S(2)}) copy-start(f32[32,8,4,36]{3,2,1,0:T(4,128)} %get-tuple-element.338) | copy-start | bytes 442372
  123.1 0.7 copy-start.4
  123.8 1.6 copy-start.2
  126.0 7.9 %collective-permute-start.1 = (f32[4,9216]{1,0:T(4,128)S(1)}, f32[4,9216]{1,0:T(4,128)S(1)}, u32[]{:S(2)}, u32[]{:S(2)}) collective-permute-start(f32[4,9216]{1,0:T(4,128)S(1)} %get-tuple-element.554), channel_id=1, source_target_pairs={{7,0},{0,1},{1,2},{2,3},{3,4},{4,5},{5,6},{6,7},{15,8},{8,9},{9,10... | collective-permute-start | bytes 442376 | tf_op jit(solution)/shard_map/while/body/eval_jaxpr/ppermute | solution.py:12
  133.9 7.9 %collective-permute-start.1 = (f32[4,9216]{1,0:T(4,128)S(1)}, f32[4,9216]{1,0:T(4,128)S(1)}, u32[]{:S(2)}, u32[]{:S(2)}) collective-permute-start(f32[4,9216]{1,0:T(4,128)S(1)} %get-tuple-element.554), channel_id=1, source_target_pairs={{7,0},{0,1},{1,2},{2,3},{3,4},{4,5},{5,6},{6,7},{15,8},{8,9},{9,10... | collective-permute-start | bytes 442376 | tf_op jit(solution)/shard_map/while/body/eval_jaxpr/ppermute | solution.py:12
  141.9 7.9 %collective-permute-start.1 = (f32[4,9216]{1,0:T(4,128)S(1)}, f32[4,9216]{1,0:T(4,128)S(1)}, u32[]{:S(2)}, u32[]{:S(2)}) collective-permute-start(f32[4,9216]{1,0:T(4,128)S(1)} %get-tuple-element.554), channel_id=1, source_target_pairs={{7,0},{0,1},{1,2},{2,3},{3,4},{4,5},{5,6},{6,7},{15,8},{8,9},{9,10... | collective-permute-start | bytes 442376 | tf_op jit(solution)/shard_map/while/body/eval_jaxpr/ppermute | solution.py:12
  149.8 8.2 %collective-permute-start.1 = (f32[4,9216]{1,0:T(4,128)S(1)}, f32[4,9216]{1,0:T(4,128)S(1)}, u32[]{:S(2)}, u32[]{:S(2)}) collective-permute-start(f32[4,9216]{1,0:T(4,128)S(1)} %get-tuple-element.554), channel_id=1, source_target_pairs={{7,0},{0,1},{1,2},{2,3},{3,4},{4,5},{5,6},{6,7},{15,8},{8,9},{9,10... | collective-permute-start | bytes 442376 | tf_op jit(solution)/shard_map/while/body/eval_jaxpr/ppermute | solution.py:12
  158.1 9.3 %collective-permute-start.1 = (f32[4,9216]{1,0:T(4,128)S(1)}, f32[4,9216]{1,0:T(4,128)S(1)}, u32[]{:S(2)}, u32[]{:S(2)}) collective-permute-start(f32[4,9216]{1,0:T(4,128)S(1)} %get-tuple-element.554), channel_id=1, source_target_pairs={{7,0},{0,1},{1,2},{2,3},{3,4},{4,5},{5,6},{6,7},{15,8},{8,9},{9,10... | collective-permute-start | bytes 442376 | tf_op jit(solution)/shard_map/while/body/eval_jaxpr/ppermute | solution.py:12
  167.5 7.9 %collective-permute-start.1 = (f32[4,9216]{1,0:T(4,128)S(1)}, f32[4,9216]{1,0:T(4,128)S(1)}, u32[]{:S(2)}, u32[]{:S(2)}) collective-permute-start(f32[4,9216]{1,0:T(4,128)S(1)} %get-tuple-element.554), channel_id=1, source_target_pairs={{7,0},{0,1},{1,2},{2,3},{3,4},{4,5},{5,6},{6,7},{15,8},{8,9},{9,10... | collective-permute-start | bytes 442376 | tf_op jit(solution)/shard_map/while/body/eval_jaxpr/ppermute | solution.py:12
  175.4 7.9 %collective-permute-start.1 = (f32[4,9216]{1,0:T(4,128)S(1)}, f32[4,9216]{1,0:T(4,128)S(1)}, u32[]{:S(2)}, u32[]{:S(2)}) collective-permute-start(f32[4,9216]{1,0:T(4,128)S(1)} %get-tuple-element.554), channel_id=1, source_target_pairs={{7,0},{0,1},{1,2},{2,3},{3,4},{4,5},{5,6},{6,7},{15,8},{8,9},{9,10... | collective-permute-start | bytes 442376 | tf_op jit(solution)/shard_map/while/body/eval_jaxpr/ppermute | solution.py:12
Sparse Core Ops, SparseCore 0:
  186.4 46.3 reduce-scatter.3
where the time goes:
time: 243 us; the launch traced here: 242 us
  waiting for transfers between devices  91.4 us (38%)
  local copies, waits for them, and re-layouts  69.9 us (29%)
  blocking collectives  37.2 us (15%)
  matrix products  17.3 us (7%)
  between operations  14.2 us (6%)
  other arithmetic  7.01 us (3%)
  starting transfers between devices  3.74 us (2%)
    ppermute x14, waiting for transfers between devices, shifted(): return lax.ppermute(block, axis, route)  83.3 us
    psum x1, blocking collectives, body(): totals = lax.psum(jnp.sum(posterior, axis=(0, 2)), ('dom', 'blk'))  37.2 us
    transpose x8, local copies, waits for them, and re-layouts, correlate(): jnp.einsum('iqj,kpj->ikqp', shaped, ref_shaped, preferred_element_type=jn...  19.3 us
    dot_general x8, local copies, waits for them, and re-layouts, correlate(): jnp.dot(flat, table, precision=lax.Precision.HIGHEST)  18.2 us
    reshape x8, local copies, waits for them, and re-layouts, contribute(): mixed = mixed.reshape(particle_count, class_width, rot_count, rot_count)  8.31 us
    unnamed x2, waiting for transfers between devices  8.14 us
    unnamed x21, local copies, waits for them, and re-layouts  7.66 us
    dot_general x8, matrix products, correlate(): jnp.dot(flat, table, precision=lax.Precision.HIGHEST)  5.49 us
  transfers between devices with their start and end apart: 15, of which 15 were waited for; matrix products, arithmetic and copies ran while one was open for 9% of the time, Pallas kernels for 0%

commit v1 on v0

v1 whole, which is shorter than its diff:
```python
import functools
import jax
import jax.numpy as jnp
from jax import lax
from jax.experimental import pallas as pl
from jax.experimental.pallas import tpu as pltpu
from jax.sharding import PartitionSpec as P

ROTS = 36
LANES = 128
F32 = jnp.float32
BF16 = jnp.bfloat16
LOW = -3.0e38
VMEM_BYTES = 24 * 1024 * 1024


def offsets(blk):
    half = blk // 2
    first = [0] + list(range(half, blk - 2 + 1))
    second = [blk - 1] + list(range(half - 1, 0, -1))
    return first, second


def routed(block, dom, blk, move):
    pairs = []
    for d in range(dom):
        for b in range(blk):
            to = move(d, b)
            if to is not None:
                pairs.append((d * blk + b, to[0] * blk + to[1]))
    return lax.ppermute(block, ("dom", "blk"), pairs)


def in_vmem(count):
    return [pl.BlockSpec(memory_space=pltpu.VMEM)] * count


def call(kernel, outs, args, scratch=(), flops=1_000_000):
    total = sum(a.size * a.dtype.itemsize for a in args) + sum(o.size * o.dtype.itemsize for o in outs)
    return pl.pallas_call(
        kernel,
        out_shape=tuple(outs),
        in_specs=in_vmem(len(args)),
        out_specs=tuple(in_vmem(len(outs))),
        scratch_shapes=list(scratch),
        compiler_params=pltpu.CompilerParams(vmem_limit_bytes=VMEM_BYTES),
        cost_estimate=pl.CostEstimate(flops=flops, bytes_accessed=total, transcendentals=0),
    )(*args)


def stack_kernel(own, other, out):
    rows, pixels = own.shape
    step = pixels // ROTS
    for q in range(ROTS):
        base = q * 2 * rows
        out[base : base + rows, :] = own[:, q * step : (q + 1) * step]
        out[base + rows : base + 2 * rows, :] = other[:, q * step : (q + 1) * step]


def pick_offset(core, pair):
    return jnp.where(core == 0, pair[0], pair[1])


def lanes_of(own, other):
    return jnp.concatenate([own, other, own, other], axis=1)


def forward_kernel(pairs, slots, *refs):
    turns = len(pairs)
    own, recv, (stacked, small_own, small_other, exps, stats, tiles, acc) = refs[0], refs[1 : 1 + turns], refs[1 + turns :]
    core = lax.axis_index("dom") & 1
    spot = lax.axis_index("blk")
    width, pixels = own.shape
    step = pixels // ROTS
    total = stacked.shape[0]
    columns = total // LANES
    rows = ROTS * width
    norms = []
    for t in range(turns):
        block = recv[t][...].astype(F32)
        if t == 0:
            block = jnp.where(core == 0, own[...].astype(F32), block)
        norms.append(jnp.sum(block * block, axis=1, keepdims=True))
        for u in range(ROTS // 4):
            tile = jnp.concatenate([block[:, (4 * u + a) * step : (4 * u + a + 1) * step] for a in range(4)], axis=0)
            tiles[t * rows + 16 * u : t * rows + 16 * (u + 1), :] = tile.astype(BF16)
    acc[...] = jnp.zeros_like(acc)
    for n in range(columns // 2):
        weights = stacked[n * 256 : (n + 1) * 256, :]
        got = lax.dot_general(tiles[...], weights, (((1,), (1,)), ((), ())), preferred_element_type=F32)
        for t in range(turns):
            for m in range(-1, columns):
                part = None
                if m >= 0:
                    part = got[t * rows + 8 * m : t * rows + 8 * m + 8, :LANES]
                if m + 1 < columns:
                    extra = got[t * rows + 8 * m + 8 : t * rows + 8 * m + 16, LANES:]
                    part = extra if part is None else part + extra
                place = ((2 * n - m) % columns) * LANES
                acc[8 * t : 8 * t + 8, place : place + LANES] += part
    corr = []
    for t in range(turns):
        odd = pltpu.roll(acc[8 * t + 4 : 8 * t + 8, :], total - 64, 1)
        corr.append(acc[8 * t : 8 * t + 4, :] + odd)
    corr = jnp.concatenate(corr, axis=0)
    norm = jnp.concatenate(norms, axis=0)
    small = lanes_of(small_own[...], small_other[...])
    inverse = small[slots : slots + 1, :]
    ids = jnp.concatenate(
        [
            lax.broadcasted_iota(jnp.int32, (width, LANES), 0) + (spot ^ pick_offset(core, pair)) * width
            for pair in pairs
        ],
        axis=0,
    ).astype(F32)
    mask = small[0:1, :] == ids
    for s in range(1, slots):
        mask = mask | (small[s : s + 1, :] == ids)
    scores = [inverse * (corr[:, c * LANES : (c + 1) * LANES] - 0.5 * norm) for c in range(columns)]
    peak = jnp.full(ids.shape, LOW, F32)
    for score in scores:
        peak = jnp.maximum(peak, score)
    peak = jnp.max(jnp.where(mask, peak, LOW), axis=0, keepdims=True)
    peak = jnp.maximum(peak, pltpu.roll(peak, 64, 1))
    mass = jnp.zeros(ids.shape, F32)
    for c, score in enumerate(scores):
        term = jnp.where(mask, jnp.exp(score - peak), 0.0)
        exps[:, c * LANES : (c + 1) * LANES] = term
        mass = mass + term
    mass = jnp.sum(mass, axis=0, keepdims=True)
    mass = mass + pltpu.roll(mass, 64, 1)
    stats[...] = jnp.concatenate([peak, mass, jnp.zeros((6, LANES), F32)], axis=0)


def backward_kernel(turns, *refs):
    exps, mine, theirs, stacked = refs[:4]
    sends, (own, evidence, left) = refs[4 : 4 + turns], refs[4 + turns :]
    total = stacked.shape[0]
    columns = total // LANES
    width = exps.shape[0] // turns
    rows = ROTS * width
    extra_rows = own.shape[0] - rows
    peak, mass = mine[0:1, :], mine[1:2, :]
    peak_far, mass_far = pltpu.roll(theirs[0:1, :], 32, 1), pltpu.roll(theirs[1:2, :], 32, 1)
    top = jnp.maximum(peak, peak_far)
    share = jnp.exp(peak - top)
    whole = mass * share + mass_far * jnp.exp(peak_far - top)
    evidence[...] = (top + jnp.log(whole))[:, : evidence.shape[1]]
    factor = share / whole
    post = jnp.concatenate([exps[:, c * LANES : (c + 1) * LANES] * factor for c in range(columns)], axis=1)
    weight = jnp.sum(post, axis=1, keepdims=True)
    turned = pltpu.roll(post, 64, 1)
    for t in range(turns):
        two = jnp.concatenate([post[width * t : width * (t + 1), :], turned[width * t : width * (t + 1), :]], axis=0)
        four = jnp.concatenate([two, pltpu.roll(two, 128, 1)], axis=0).astype(BF16)
        for u in range(ROTS // 4):
            cut = total - 256 * u
            rotated = four if u == 0 else jnp.concatenate([four[:, cut:], four[:, :cut]], axis=1)
            left[t * rows + 16 * u : t * rows + 16 * (u + 1), :] = rotated
    result = jnp.dot(left[...], stacked[...], preferred_element_type=F32)
    lane = lax.broadcasted_iota(jnp.int32, (extra_rows, own.shape[1]), 1)
    row = lax.broadcasted_iota(jnp.int32, (extra_rows, own.shape[1]), 0)
    for t in range(turns):
        piece = weight[width * t : width * (t + 1), :]
        piece = jnp.concatenate([piece, jnp.zeros((extra_rows - width, 1), F32)], axis=0)
        block = result[t * rows : (t + 1) * rows, :]
        high = piece.astype(BF16).astype(F32)
        middle = (piece - high).astype(BF16).astype(F32)
        low = piece - high - middle
        if t == 0:
            own[:rows, :] = block
            own[rows:, :] = jnp.where(lane == 0, piece, 0.0)
        sends[t][:rows, :] = block.astype(BF16)
        sends[t][rows:, :] = jnp.where(
            lane == 0, high, jnp.where(lane == 1, middle, jnp.where(lane == 2, low, 0.0))
        ).astype(BF16)


def gather_kernel(turns, width, *refs):
    own, recv, outs, split = refs[0], refs[1 : 1 + turns], refs[1 + turns : -1], refs[-1]
    shards = len(outs)
    me = lax.axis_index("dom")
    rows = ROTS * width
    part = rows // shards
    value = recv[0][...].astype(F32)
    value = jnp.where((me & 1) == 0, own[...], value)
    for t in range(1, turns):
        value = value + recv[t][...].astype(F32)
    weight = jnp.sum(value[rows : rows + width, :], axis=1, keepdims=True)
    weight = jnp.broadcast_to(weight, (width, value.shape[1]))
    for s in range(shards):
        split[s, :, :] = jnp.concatenate([value[s * part : (s + 1) * part, :], weight], axis=0)
    for s in range(shards):
        outs[s][...] = split[me ^ s]


def finish_kernel(width, *refs):
    parts, (sums, weights) = refs[:-2], refs[-2:]
    value = parts[0][...]
    for part in parts[1:]:
        value = value + part[...]
    step = value.shape[1]
    chunks = value.shape[0] // width - 1
    for c in range(chunks):
        sums[:, c * step : (c + 1) * step] = value[c * width : (c + 1) * width, :]
    tail = value[chunks * width :, :LANES]
    pick = lax.broadcasted_iota(jnp.int32, tail.shape, 0) == lax.broadcasted_iota(jnp.int32, tail.shape, 1)
    weights[...] = jnp.sum(jnp.where(pick, tail, 0.0), axis=0, keepdims=True)[:, : weights.shape[1]]


def body(particles, references, inv_noise, significant, sig_count):
    dom, blk = lax.axis_size("dom"), lax.axis_size("blk")
    count, pixels = particles.shape
    width = references.shape[0]
    slots = significant.shape[1]
    step = pixels // ROTS
    first, second = offsets(blk)
    pairs = list(zip(first, second))
    turns = len(pairs)
    total = ROTS * 2 * count
    shape = jax.ShapeDtypeStruct

    def over_blk(block, pair):
        def move(d, b):
            by = pair[d & 1]
            return None if by == 0 else (d, b ^ by)

        return routed(block, dom, blk, move)

    def over_dom(block, by):
        return routed(block, dom, blk, lambda d, b: (d ^ by, b))

    recv = [over_blk(references, pair) for pair in pairs]
    other = over_dom(particles, 1)
    live = lax.broadcasted_iota(jnp.int32, (slots, count), 0) < sig_count[None, :]
    small = jnp.concatenate(
        [
            jnp.where(live, significant.T, -1).astype(F32),
            inv_noise[None, :],
            jnp.zeros((7, count), F32),
        ],
        axis=0,
    )
    small_other = over_dom(small, 1)
    (stacked,) = call(stack_kernel, [shape((total, step), BF16)], [particles, other])
    exps, stats = call(
        functools.partial(forward_kernel, pairs, slots),
        [shape((turns * width, total), F32), shape((8, LANES), F32)],
        [references, *recv, stacked, small, small_other],
        [pltpu.VMEM((turns * ROTS * width, step), BF16), pltpu.VMEM((turns * 8, total), F32)],
    )
    stats_other = over_dom(stats, 1)
    rows = ROTS * width
    *sends, own, evidence = call(
        functools.partial(backward_kernel, turns),
        [shape((rows + 16, step), BF16)] * turns + [shape((rows + 16, step), F32), shape((1, count), F32)],
        [exps, stats, stats_other, stacked],
        [pltpu.VMEM((turns * rows, total), BF16)],
    )
    recv = [over_blk(block, pair) for block, pair in zip(sends, pairs)]
    parts = call(
        functools.partial(gather_kernel, turns, width),
        [shape((rows // dom + width, step), F32)] * dom,
        [own, *recv],
        [pltpu.VMEM((dom, rows // dom + width, step), F32)],
    )
    parts = [parts[0]] + [over_dom(parts[s], s) for s in range(1, dom)]
    sums, weights = call(
        functools.partial(finish_kernel, width),
        [shape((width, pixels // dom), F32), shape((1, width), F32)],
        parts,
    )
    return sums, weights.reshape(width), evidence.reshape(count)


def solution(mesh):
    in_specs = (
        P(("dom", "blk"), None),
        P("blk", None),
        P(("dom", "blk")),
        P(("dom", "blk"), None),
        P(("dom", "blk")),
    )
    out_specs = (P("blk", "dom"), P("blk"), P(("dom", "blk")))
    return jax.shard_map(body, mesh=mesh, in_specs=in_specs, out_specs=out_specs, check_vma=False)
```

time: 243 us -> 36.5 us (0.15)
  waiting for transfers between devices: 91.4 us -> 10.3 us
  local copies, waits for them, and re-layouts: 69.9 us -> 1.89 us
  blocking collectives: 37.2 us -> 0 us
  matrix products: 17.3 us -> 0 us
  starting transfers between devices: 3.74 us -> 18.9 us
  between operations: 14.2 us -> 0.72 us
  other arithmetic: 7.01 us -> 1.42 us
  Pallas kernels: 0 us -> 3.08 us
    ppermute x14, waiting for transfers between devices: 83.3 us -> 10.3 us  [routed(): return lax.ppermute(block, ('dom', 'blk'), pairs)]
    psum x1 -> x0, blocking collectives: 37.2 us -> none  [body(): totals = lax.psum(jnp.sum(posterior, axis=(0, 2)), ('dom', 'blk'))]
    transpose x8 -> x0, local copies, waits for them, and re-layouts: 19.3 us -> none  [correlate(): jnp.einsum('iqj,kpj->ikqp', shaped, ref_shaped, preferred_element_type=jn...]
    dot_general x8 -> x0, local copies, waits for them, and re-layouts: 18.2 us -> none  [correlate(): jnp.dot(flat, table, precision=lax.Precision.HIGHEST)]
    dot_general x32 -> x0, matrix products: 17.3 us -> none  [the longest x8 5.49 us: correlate(): jnp.dot(flat, table, precision=lax.Precision.HIGHEST)]
    ppermute x14, starting transfers between devices: 3.7 us -> 18.9 us  [routed(): return lax.ppermute(block, ('dom', 'blk'), pairs)]
    reshape x18 -> x0, local copies, waits for them, and re-layouts: 11.2 us -> none  [the longest x8 8.31 us: contribute(): mixed = mixed.reshape(particle_count, class_width, rot_count, rot_count)]
    unnamed x2 -> x0, waiting for transfers between devices: 8.14 us -> none
  transfers between devices with their start and end apart: 15 -> 14, of which waited for: 15 -> 6; matrix products, arithmetic and copies ran while one was open for 9% -> 4% of each run, Pallas kernels for 0% -> 0%
where the time goes in v1:
time: 36.5 us; the launch traced here: 36.3 us
  starting transfers between devices  18.9 us (52%)
  waiting for transfers between devices  10.3 us (28%)
  Pallas kernels  3.08 us (8%)
  local copies, waits for them, and re-layouts  1.89 us (5%)
  other arithmetic  1.42 us (4%)
  between operations  0.72 us (2%)
    ppermute x14, starting transfers between devices, routed(): return lax.ppermute(block, ('dom', 'blk'), pairs)  18.9 us
    ppermute x14, waiting for transfers between devices, routed(): return lax.ppermute(block, ('dom', 'blk'), pairs)  10.3 us
    pallas_call x5, Pallas kernels, call(): pl.pallas_call(kernel, out_shape=tuple(outs), in_specs=in_vmem(len(args))...  3.08 us
    unnamed x4, local copies, waits for them, and re-layouts  1.81 us
  transfers between devices with their start and end apart: 14, of which 6 were waited for; matrix products, arithmetic and copies ran while one was open for 4% of the time, Pallas kernels for 0%

profile of v1, /device:TPU:0, one launch (start us, length us, event | category | flops | bytes accessed | tf_op | source)
XLA Modules:
  0.0 36.3 jit_solution(15750371345153913578)
XLA Ops:
  0.6 0.5 %collective-permute-start.4 = (bf16[32,9216]{1,0:T(8,128)(2,1)}, bf16[32,9216]{1,0:T(8,128)(2,1)S(1)}, u32[]{:S(2)}, u32[]{:S(2)}) collective-permute-start(bf16[32,9216]{1,0:T(8,128)(2,1)} %own.1), channel_id=1, source_target_pairs={{0,8},{1,9},{2,10},{3,11},{4,12},{5,13},{6,14},{7,15},{8,0},{9,1},... | collective-permute-start | bytes 1769480 | tf_op jit(solution)/shard_map/ppermute | solution.py:31
  1.1 0.7 %collective-permute-start = (bf16[4,9216]{1,0:T(4,128)(2,1)}, bf16[4,9216]{1,0:T(4,128)(2,1)S(1)}, u32[]{:S(2)}, u32[]{:S(2)}) collective-permute-start(bf16[4,9216]{1,0:T(4,128)(2,1)} %refs_0_.1), channel_id=1, source_target_pairs={{8,15},{9,14},{10,13},{11,12},{12,11},{13,10},{14,9},{15,8},{24,31... | collective-permute-start | bytes 221192 | tf_op jit(solution)/shard_map/ppermute | solution.py:31
  1.8 3.7 %collective-permute-start.1 = (bf16[4,9216]{1,0:T(4,128)(2,1)}, bf16[4,9216]{1,0:T(4,128)(2,1)S(1)}, u32[]{:S(2)}, u32[]{:S(2)}) collective-permute-start(bf16[4,9216]{1,0:T(4,128)(2,1)} %refs_0_.1), channel_id=1, source_target_pairs={{0,4},{1,5},{2,6},{3,7},{4,0},{5,1},{6,2},{7,3},{8,11},{9,10},{10,... | collective-permute-start | bytes 221192 | tf_op jit(solution)/shard_map/ppermute | solution.py:31
  5.5 1.3 %collective-permute-start.2 = (bf16[4,9216]{1,0:T(4,128)(2,1)}, bf16[4,9216]{1,0:T(4,128)(2,1)S(1)}, u32[]{:S(2)}, u32[]{:S(2)}) collective-permute-start(bf16[4,9216]{1,0:T(4,128)(2,1)} %refs_0_.1), channel_id=1, source_target_pairs={{0,5},{1,4},{2,7},{3,6},{4,1},{5,0},{6,3},{7,2},{8,10},{9,11},{10,... | collective-permute-start | bytes 221192 | tf_op jit(solution)/shard_map/ppermute | solution.py:31
  6.7 3.6 %collective-permute-start.3 = (bf16[4,9216]{1,0:T(4,128)(2,1)}, bf16[4,9216]{1,0:T(4,128)(2,1)S(1)}, u32[]{:S(2)}, u32[]{:S(2)}) collective-permute-start(bf16[4,9216]{1,0:T(4,128)(2,1)} %refs_0_.1), channel_id=1, source_target_pairs={{0,6},{1,7},{2,4},{3,5},{4,2},{5,3},{6,0},{7,1},{8,9},{9,8},{10,11... | collective-permute-start | bytes 221192 | tf_op jit(solution)/shard_map/ppermute | solution.py:31
  10.4 0.1 pad.2.clone
  10.4 0.7 %fusion = f32[8,32]{1,0:T(8,128)S(1)} fusion(s32[32,8]{0,1:T(8,128)} %param.8, s32[32]{0:T(128)} %param.9), kind=kLoop, calls=%fused_computation.2 | loop fusion | flops 768 | bytes 2176 | tf_op jit(solution)/shard_map/convert_element_type | solution.py:238
  11.1 0.7 %maximum_maximum_fusion.refs_6_ = f32[16,32]{1,0:T(8,128)S(1)} fusion(f32[1,32]{1,0:T(1,128)} %bitcast.7, f32[8,32]{1,0:T(8,128)S(1)} %fusion, f32[16]{0:T(128)S(1)} %pad.2.clone), kind=kLoop, calls=%fused_computation | loop fusion | flops 1024 | bytes 3264 | tf_op jit(solution)/shard_map/concatenate | solution.py:236
  11.9 0.0 collective-permute-done.4.other
  11.9 1.2 %collective-permute-start.5 = (f32[16,32]{1,0:T(8,128)S(1)}, f32[16,32]{1,0:T(8,128)S(1)}, u32[]{:S(2)}, u32[]{:S(2)}) collective-permute-start(f32[16,32]{1,0:T(8,128)S(1)} %maximum_maximum_fusion.refs_6_), channel_id=1, source_target_pairs={{0,8},{1,9},{2,10},{3,11},{4,12},{5,13},{6,14},{7,15},{8,0},{9,1},... | collective-permute-start | bytes 6152 | tf_op jit(solution)/shard_map/ppermute | solution.py:31
  13.0 1.1 %copy-done = bf16[32,9216]{1,0:T(8,128)(2,1)S(1)} copy-done((bf16[32,9216]{1,0:T(8,128)(2,1)S(1)}, bf16[32,9216]{1,0:T(8,128)(2,1)}, u32[]{:S(2)}) %copy-start) | copy-done | bytes 589848
  14.1 0.1 shard_map.76.refs_5_.refs_3_
  14.2 0.0 collective-permute-done.5.refs_7_
  14.2 0.7 %copy-done.1 = bf16[4,9216]{1,0:T(4,128)(2,1)S(1)} copy-done((bf16[4,9216]{1,0:T(4,128)(2,1)S(1)}, bf16[4,9216]{1,0:T(4,128)(2,1)}, u32[]{:S(2)}) %copy-start.1) | copy-done | bytes 73752
  15.0 1.3 %shard_map.77 = (f32[16,2304]{1,0:T(8,128)S(1)}, f32[8,128]{1,0:T(8,128)S(1)}) custom-call(bf16[4,9216]{1,0:T(4,128)(2,1)S(1)} %copy-done.1, bf16[4,9216]{1,0:T(4,128)(2,1)S(1)} %collective-permute-done.refs_1_, bf16[4,9216]{1,0:T(4,128)(2,1)S(1)} %collective-permute-done.1.refs_2_, bf16[4,9216]{1,0:T(4,128)(2,1)S(1)} %collective-permute-done.2.refs_3_, ...), custom_call_target="tpu_custom_call" | custom-call | flops 1000000 | bytes 1703936 | tf_op jit(solution)/shard_map/pallas_call | solution.py:40
  16.2 0.0 collective-permute-start.6
  16.3 1.2 %collective-permute-done.6.refs_2_ = f32[8,128]{1,0:T(8,128)S(1)} collective-permute-done((f32[8,128]{1,0:T(8,128)S(1)}, f32[8,128]{1,0:T(8,128)S(1)}, u32[]{:S(2)}, u32[]{:S(2)}) %collective-permute-start.6) | collective-permute-done | bytes 4128 | tf_op jit(solution)/shard_map/ppermute | solution.py:31
  17.4 1.0 %shard_map.78 = (bf16[160,256]{1,0:T(8,128)(2,1)S(1)}, bf16[160,256]{1,0:T(8,128)(2,1)S(1)}, bf16[160,256]{1,0:T(8,128)(2,1)S(1)}, bf16[160,256]{1,0:T(8,128)(2,...) custom-call(f32[16,2304]{1,0:T(8,128)S(1)} %get-tuple-element.17.refs_0_, f32[8,128]{1,0:T(8,128)S(1)} %get-tuple-element.18.refs_1_, ...), custom_call_target="tpu_custom_call" | custom-call | flops 1000000 | bytes 1826944 | tf_op jit(solution)/shard_map/pallas_call | solution.py:40
  18.4 2.4 %collective-permute-start.10 = (bf16[160,256]{1,0:T(8,128)(2,1)S(1)}, bf16[160,256]{1,0:T(8,128)(2,1)S(1)}, u32[]{:S(2)}, u32[]{:S(2)}) collective-permute-start(bf16[160,256]{1,0:T(8,128)(2,1)S(1)} %get-tuple-element.23), channel_id=1, source_target_pairs={{0,6},{1,7},{2,4},{3,5},{4,2},{5,3},{6,0},{7,1},{8,9},{9,8},{10,11... | collective-permute-start | bytes 245768 | tf_op jit(solution)/shard_map/ppermute | solution.py:31
  20.8 0.7 %collective-permute-start.7 = (bf16[160,256]{1,0:T(8,128)(2,1)S(1)}, bf16[160,256]{1,0:T(8,128)(2,1)S(1)}, u32[]{:S(2)}, u32[]{:S(2)}) collective-permute-start(bf16[160,256]{1,0:T(8,128)(2,1)S(1)} %get-tuple-element.20), channel_id=1, source_target_pairs={{8,15},{9,14},{10,13},{11,12},{12,11},{13,10},{14,9},{15,8},{24,31... | collective-permute-start | bytes 245768 | tf_op jit(solution)/shard_map/ppermute | solution.py:31
  21.5 0.1 collective-permute-start.8
  21.5 2.9 %collective-permute-start.9 = (bf16[160,256]{1,0:T(8,128)(2,1)S(1)}, bf16[160,256]{1,0:T(8,128)(2,1)S(1)}, u32[]{:S(2)}, u32[]{:S(2)}) collective-permute-start(bf16[160,256]{1,0:T(8,128)(2,1)S(1)} %get-tuple-element.22), channel_id=1, source_target_pairs={{0,5},{1,4},{2,7},{3,6},{4,1},{5,0},{6,3},{7,2},{8,10},{9,11},{10,... | collective-permute-start | bytes 245768 | tf_op jit(solution)/shard_map/ppermute | solution.py:31
  24.4 0.3 collective-permute-done.10.refs_4_
  24.8 4.1 %collective-permute-done.8.refs_2_ = bf16[160,256]{1,0:T(8,128)(2,1)S(1)} collective-permute-done((bf16[160,256]{1,0:T(8,128)(2,1)S(1)}, bf16[160,256]{1,0:T(8,128)(2,1)S(1)}, u32[]{:S(2)}, u32[]{:S(2)}) %collective-permute-start.8) | collective-permute-done | bytes 81952 | tf_op jit(solution)/shard_map/ppermute | solution.py:31
  28.9 1.3 %collective-permute-done.9.refs_3_ = bf16[160,256]{1,0:T(8,128)(2,1)S(1)} collective-permute-done((bf16[160,256]{1,0:T(8,128)(2,1)S(1)}, bf16[160,256]{1,0:T(8,128)(2,1)S(1)}, u32[]{:S(2)}, u32[]{:S(2)}) %collective-permute-start.9) | collective-permute-done | bytes 81952 | tf_op jit(solution)/shard_map/ppermute | solution.py:31
  30.3 0.1 shard_map.79
  30.4 0.2 collective-permute-start.11
  30.6 1.5 %collective-permute-start.12 = (f32[40,256]{1,0:T(8,128)S(1)}, f32[40,256]{1,0:T(8,128)S(1)}, u32[]{:S(2)}, u32[]{:S(2)}) collective-permute-start(f32[40,256]{1,0:T(8,128)S(1)} %get-tuple-element.26), channel_id=1, source_target_pairs={{0,16},{1,17},{2,18},{3,19},{4,20},{5,21},{6,22},{7,23},{8,24},{9,... | collective-permute-start | bytes 122888 | tf_op jit(solution)/shard_map/ppermute | solution.py:31
  32.1 0.3 collective-permute-start.13
  32.4 2.2 %collective-permute-done.12.refs_2_ = f32[40,256]{1,0:T(8,128)S(1)} collective-permute-done((f32[40,256]{1,0:T(8,128)S(1)}, f32[40,256]{1,0:T(8,128)S(1)}, u32[]{:S(2)}, u32[]{:S(2)}) %collective-permute-start.12) | collective-permute-done | bytes 40992 | tf_op jit(solution)/shard_map/ppermute | solution.py:31
  34.6 1.1 %collective-permute-done.13.refs_3_ = f32[40,256]{1,0:T(8,128)S(1)} collective-permute-done((f32[40,256]{1,0:T(8,128)S(1)}, f32[40,256]{1,0:T(8,128)S(1)}, u32[]{:S(2)}, u32[]{:S(2)}) %collective-permute-start.13) | collective-permute-done | bytes 40992 | tf_op jit(solution)/shard_map/ppermute | solution.py:31
  35.6 0.6 %shard_map.80 = (f32[4,2304]{1,0:T(4,128)}, f32[1,4]{1,0:T(1,128)}) custom-call(f32[40,256]{1,0:T(8,128)S(1)} %get-tuple-element.24.refs_0_, f32[40,256]{1,0:T(8,128)S(1)} %collective-permute-done.11.refs_1_, f32[40,256]{1,0:T(8,128)S(1)} %collective-permute-done.12.refs_2_, f32[40,256]{1,0:T(8,128)S(1)} %collective-permute-done.13.refs_3_), custom_call_target="tpu_custom_call" | custom-call | flops 1000000 | bytes 200720 | tf_op jit(solution)/shard_map/pallas_call | solution.py:40
  (9 shorter events, 0.0 us)
Async XLA Ops:
  0.6 11.2 %collective-permute-start.4 = (bf16[32,9216]{1,0:T(8,128)(2,1)}, bf16[32,9216]{1,0:T(8,128)(2,1)S(1)}, u32[]{:S(2)}, u32[]{:S(2)}) collective-permute-start(bf16[32,9216]{1,0:T(8,128)(2,1)} %own.1), channel_id=1, source_target_pairs={{0,8},{1,9},{2,10},{3,11},{4,12},{5,13},{6,14},{7,15},{8,0},{9,1},... | collective-permute-start | bytes 1769480 | tf_op jit(solution)/shard_map/ppermute | solution.py:31
  1.1 13.0 %collective-permute-start = (bf16[4,9216]{1,0:T(4,128)(2,1)}, bf16[4,9216]{1,0:T(4,128)(2,1)S(1)}, u32[]{:S(2)}, u32[]{:S(2)}) collective-permute-start(bf16[4,9216]{1,0:T(4,128)(2,1)} %refs_0_.1), channel_id=1, source_target_pairs={{8,15},{9,14},{10,13},{11,12},{12,11},{13,10},{14,9},{15,8},{24,31... | collective-permute-start | bytes 221192 | tf_op jit(solution)/shard_map/ppermute | solution.py:31
  1.8 12.4 %collective-permute-start.1 = (bf16[4,9216]{1,0:T(4,128)(2,1)}, bf16[4,9216]{1,0:T(4,128)(2,1)S(1)}, u32[]{:S(2)}, u32[]{:S(2)}) collective-permute-start(bf16[4,9216]{1,0:T(4,128)(2,1)} %refs_0_.1), channel_id=1, source_target_pairs={{0,4},{1,5},{2,6},{3,7},{4,0},{5,1},{6,2},{7,3},{8,11},{9,10},{10,... | collective-permute-start | bytes 221192 | tf_op jit(solution)/shard_map/ppermute | solution.py:31
  5.5 8.7 %collective-permute-start.2 = (bf16[4,9216]{1,0:T(4,128)(2,1)}, bf16[4,9216]{1,0:T(4,128)(2,1)S(1)}, u32[]{:S(2)}, u32[]{:S(2)}) collective-permute-start(bf16[4,9216]{1,0:T(4,128)(2,1)} %refs_0_.1), channel_id=1, source_target_pairs={{0,5},{1,4},{2,7},{3,6},{4,1},{5,0},{6,3},{7,2},{8,10},{9,11},{10,... | collective-permute-start | bytes 221192 | tf_op jit(solution)/shard_map/ppermute | solution.py:31
  6.7 7.5 %collective-permute-start.3 = (bf16[4,9216]{1,0:T(4,128)(2,1)}, bf16[4,9216]{1,0:T(4,128)(2,1)S(1)}, u32[]{:S(2)}, u32[]{:S(2)}) collective-permute-start(bf16[4,9216]{1,0:T(4,128)(2,1)} %refs_0_.1), channel_id=1, source_target_pairs={{0,6},{1,7},{2,4},{3,5},{4,2},{5,3},{6,0},{7,1},{8,9},{9,8},{10,11... | collective-permute-start | bytes 221192 | tf_op jit(solution)/shard_map/ppermute | solution.py:31
  11.9 2.3 %collective-permute-start.5 = (f32[16,32]{1,0:T(8,128)S(1)}, f32[16,32]{1,0:T(8,128)S(1)}, u32[]{:S(2)}, u32[]{:S(2)}) collective-permute-start(f32[16,32]{1,0:T(8,128)S(1)} %maximum_maximum_fusion.refs_6_), channel_id=1, source_target_pairs={{0,8},{1,9},{2,10},{3,11},{4,12},{5,13},{6,14},{7,15},{8,0},{9,1},... | collective-permute-start | bytes 6152 | tf_op jit(solution)/shard_map/ppermute | solution.py:31
  13.0 1.1 %copy-start = (bf16[32,9216]{1,0:T(8,128)(2,1)S(1)}, bf16[32,9216]{1,0:T(8,128)(2,1)}, u32[]{:S(2)}) copy-start(bf16[32,9216]{1,0:T(8,128)(2,1)} %own.1) | copy-start | bytes 1769476
  14.1 0.9 %copy-start.1 = (bf16[4,9216]{1,0:T(4,128)(2,1)S(1)}, bf16[4,9216]{1,0:T(4,128)(2,1)}, u32[]{:S(2)}) copy-start(bf16[4,9216]{1,0:T(4,128)(2,1)} %refs_0_.1) | copy-start | bytes 221188
  16.2 1.2 %collective-permute-start.6 = (f32[8,128]{1,0:T(8,128)S(1)}, f32[8,128]{1,0:T(8,128)S(1)}, u32[]{:S(2)}, u32[]{:S(2)}) collective-permute-start(f32[8,128]{1,0:T(8,128)S(1)} %get-tuple-element.18.refs_1_), channel_id=1, source_target_pairs={{0,8},{1,9},{2,10},{3,11},{4,12},{5,13},{6,14},{7,15},{8,0},{9,1},... | collective-permute-start | bytes 12296 | tf_op jit(solution)/shard_map/ppermute | solution.py:31
  18.4 6.4 %collective-permute-start.10 = (bf16[160,256]{1,0:T(8,128)(2,1)S(1)}, bf16[160,256]{1,0:T(8,128)(2,1)S(1)}, u32[]{:S(2)}, u32[]{:S(2)}) collective-permute-start(bf16[160,256]{1,0:T(8,128)(2,1)S(1)} %get-tuple-element.23), channel_id=1, source_target_pairs={{0,6},{1,7},{2,4},{3,5},{4,2},{5,3},{6,0},{7,1},{8,9},{9,8},{10,11... | collective-permute-start | bytes 245768 | tf_op jit(solution)/shard_map/ppermute | solution.py:31
  20.8 4.0 %collective-permute-start.7 = (bf16[160,256]{1,0:T(8,128)(2,1)S(1)}, bf16[160,256]{1,0:T(8,128)(2,1)S(1)}, u32[]{:S(2)}, u32[]{:S(2)}) collective-permute-start(bf16[160,256]{1,0:T(8,128)(2,1)S(1)} %get-tuple-element.20), channel_id=1, source_target_pairs={{8,15},{9,14},{10,13},{11,12},{12,11},{13,10},{14,9},{15,8},{24,31... | collective-permute-start | bytes 245768 | tf_op jit(solution)/shard_map/ppermute | solution.py:31
  21.5 7.5 %collective-permute-start.8 = (bf16[160,256]{1,0:T(8,128)(2,1)S(1)}, bf16[160,256]{1,0:T(8,128)(2,1)S(1)}, u32[]{:S(2)}, u32[]{:S(2)}) collective-permute-start(bf16[160,256]{1,0:T(8,128)(2,1)S(1)} %get-tuple-element.21), channel_id=1, source_target_pairs={{0,4},{1,5},{2,6},{3,7},{4,0},{5,1},{6,2},{7,3},{8,11},{9,10},{10,... | collective-permute-start | bytes 245768 | tf_op jit(solution)/shard_map/ppermute | solution.py:31
  21.5 8.7 %collective-permute-start.9 = (bf16[160,256]{1,0:T(8,128)(2,1)S(1)}, bf16[160,256]{1,0:T(8,128)(2,1)S(1)}, u32[]{:S(2)}, u32[]{:S(2)}) collective-permute-start(bf16[160,256]{1,0:T(8,128)(2,1)S(1)} %get-tuple-element.22), channel_id=1, source_target_pairs={{0,5},{1,4},{2,7},{3,6},{4,1},{5,0},{6,3},{7,2},{8,10},{9,11},{10,... | collective-permute-start | bytes 245768 | tf_op jit(solution)/shard_map/ppermute | solution.py:31
  30.4 2.0 %collective-permute-start.11 = (f32[40,256]{1,0:T(8,128)S(1)}, f32[40,256]{1,0:T(8,128)S(1)}, u32[]{:S(2)}, u32[]{:S(2)}) collective-permute-start(f32[40,256]{1,0:T(8,128)S(1)} %get-tuple-element.25), channel_id=1, source_target_pairs={{0,8},{1,9},{2,10},{3,11},{4,12},{5,13},{6,14},{7,15},{8,0},{9,1},... | collective-permute-start | bytes 122888 | tf_op jit(solution)/shard_map/ppermute | solution.py:31
  30.6 4.0 %collective-permute-start.12 = (f32[40,256]{1,0:T(8,128)S(1)}, f32[40,256]{1,0:T(8,128)S(1)}, u32[]{:S(2)}, u32[]{:S(2)}) collective-permute-start(f32[40,256]{1,0:T(8,128)S(1)} %get-tuple-element.26), channel_id=1, source_target_pairs={{0,16},{1,17},{2,18},{3,19},{4,20},{5,21},{6,22},{7,23},{8,24},{9,... | collective-permute-start | bytes 122888 | tf_op jit(solution)/shard_map/ppermute | solution.py:31
  32.1 3.5 %collective-permute-start.13 = (f32[40,256]{1,0:T(8,128)S(1)}, f32[40,256]{1,0:T(8,128)S(1)}, u32[]{:S(2)}, u32[]{:S(2)}) collective-permute-start(f32[40,256]{1,0:T(8,128)S(1)} %get-tuple-element.27), channel_id=1, source_target_pairs={{0,24},{1,25},{2,26},{3,27},{4,28},{5,29},{6,30},{7,31},{8,16},{9,... | collective-permute-start | bytes 122888 | tf_op jit(solution)/shard_map/ppermute | solution.py:31

commit v2 on v1

--- a/solution.py
+++ b/solution.py
@@ -16,9 +16,11 @@
 
 def offsets(blk):
     half = blk // 2
-    first = [0] + list(range(half, blk - 2 + 1))
+    first = list(range(half, blk - 1)) + [0]
     second = [blk - 1] + list(range(half - 1, 0, -1))
-    return first, second
+    pairs = list(zip(first, second))
+    order = list(range(1, half)) + [0]
+    return pairs, order
 
 
 def routed(block, dom, blk, move):
@@ -31,17 +33,14 @@
     return lax.ppermute(block, ("dom", "blk"), pairs)
 
 
-def in_vmem(count):
-    return [pl.BlockSpec(memory_space=pltpu.VMEM)] * count
-
-
 def call(kernel, outs, args, scratch=(), flops=1_000_000):
     total = sum(a.size * a.dtype.itemsize for a in args) + sum(o.size * o.dtype.itemsize for o in outs)
+    near = pl.BlockSpec(memory_space=pltpu.VMEM)
     return pl.pallas_call(
         kernel,
         out_shape=tuple(outs),
-        in_specs=in_vmem(len(args)),
-        out_specs=tuple(in_vmem(len(outs))),
+        in_specs=[near] * len(args),
+        out_specs=tuple([near] * len(outs)),
         scratch_shapes=list(scratch),
         compiler_params=pltpu.CompilerParams(vmem_limit_bytes=VMEM_BYTES),
         cost_estimate=pl.CostEstimate(flops=flops, bytes_accessed=total, transcendentals=0),
@@ -65,12 +64,15 @@
     return jnp.concatenate([own, other, own, other], axis=1)
 
 
-def forward_kernel(pairs, slots, *refs):
+def forward_kernel(pairs, *refs):
     turns = len(pairs)
-    own, recv, (stacked, small_own, small_other, exps, stats, tiles, acc) = refs[0], refs[1 : 1 + turns], refs[1 + turns :]
+    recv = refs[:turns]
+    stacked, lists_own, lists_other, exps, stats, tiles, acc = refs[turns:]
     core = lax.axis_index("dom") & 1
     spot = lax.axis_index("blk")
-    width, pixels = own.shape
+    width, pixels = recv[0].shape
+    slots = lists_own.shape[0] // 2
+    lists = lanes_of(lists_own[...], lists_other[...])
     step = pixels // ROTS
     total = stacked.shape[0]
     columns = total // LANES
@@ -78,8 +80,6 @@
     norms = []
     for t in range(turns):
         block = recv[t][...].astype(F32)
-        if t == 0:
-            block = jnp.where(core == 0, own[...].astype(F32), block)
         norms.append(jnp.sum(block * block, axis=1, keepdims=True))
         for u in range(ROTS // 4):
             tile = jnp.concatenate([block[:, (4 * u + a) * step : (4 * u + a + 1) * step] for a in range(4)], axis=0)
@@ -104,8 +104,7 @@
         corr.append(acc[8 * t : 8 * t + 4, :] + odd)
     corr = jnp.concatenate(corr, axis=0)
     norm = jnp.concatenate(norms, axis=0)
-    small = lanes_of(small_own[...], small_other[...])
-    inverse = small[slots : slots + 1, :]
+    inverse = lists[slots : slots + 1, :]
     ids = jnp.concatenate(
         [
             lax.broadcasted_iota(jnp.int32, (width, LANES), 0) + (spot ^ pick_offset(core, pair)) * width
@@ -113,9 +112,9 @@
         ],
         axis=0,
     ).astype(F32)
-    mask = small[0:1, :] == ids
+    mask = lists[0:1, :] == ids
     for s in range(1, slots):
-        mask = mask | (small[s : s + 1, :] == ids)
+        mask = mask | (lists[s : s + 1, :] == ids)
     scores = [inverse * (corr[:, c * LANES : (c + 1) * LANES] - 0.5 * norm) for c in range(columns)]
     peak = jnp.full(ids.shape, LOW, F32)
     for score in scores:
@@ -132,7 +131,8 @@
     stats[...] = jnp.concatenate([peak, mass, jnp.zeros((6, LANES), F32)], axis=0)
 
 
-def backward_kernel(turns, *refs):
+def backward_kernel(pairs, *refs):
+    turns = len(pairs)
     exps, mine, theirs, stacked = refs[:4]
     sends, (own, evidence, left) = refs[4 : 4 + turns], refs[4 + turns :]
     total = stacked.shape[0]
@@ -167,31 +167,41 @@
         high = piece.astype(BF16).astype(F32)
         middle = (piece - high).astype(BF16).astype(F32)
         low = piece - high - middle
-        if t == 0:
+        if pairs[t][0] == 0:
             own[:rows, :] = block
             own[rows:, :] = jnp.where(lane == 0, piece, 0.0)
-        sends[t][:rows, :] = block.astype(BF16)
-        sends[t][rows:, :] = jnp.where(
-            lane == 0, high, jnp.where(lane == 1, middle, jnp.where(lane == 2, low, 0.0))
-        ).astype(BF16)
-
-
-def gather_kernel(turns, width, *refs):
-    own, recv, outs, split = refs[0], refs[1 : 1 + turns], refs[1 + turns : -1], refs[-1]
-    shards = len(outs)
-    me = lax.axis_index("dom")
+        tail = jnp.where(lane == 0, high, jnp.where(lane == 1, middle, jnp.where(lane == 2, low, 0.0)))
+        sends[t][...] = jnp.concatenate([block, tail], axis=0).astype(BF16)
+
+
+def gather_kernel(pairs, width, *refs):
+    turns = len(pairs)
+    own, recv, (keep, give) = refs[0], refs[1 : 1 + turns], refs[1 + turns :]
+    core = lax.axis_index("dom") & 1
     rows = ROTS * width
-    part = rows // shards
-    value = recv[0][...].astype(F32)
-    value = jnp.where((me & 1) == 0, own[...], value)
-    for t in range(1, turns):
-        value = value + recv[t][...].astype(F32)
+    sides = keep.shape[0]
+    part = rows // (2 * sides)
+    value = None
+    for t in range(turns):
+        block = recv[t][...].astype(F32)
+        if pairs[t][0] == 0:
+            block = jnp.where(core == 0, own[...], block)
+        value = block if value is None else value + block
     weight = jnp.sum(value[rows : rows + width, :], axis=1, keepdims=True)
     weight = jnp.broadcast_to(weight, (width, value.shape[1]))
-    for s in range(shards):
-        split[s, :, :] = jnp.concatenate([value[s * part : (s + 1) * part, :], weight], axis=0)
-    for s in range(shards):
-        outs[s][...] = split[me ^ s]
+    for s in range(sides):
+        one = value[2 * s * part : (2 * s + 1) * part, :]
+        two = value[(2 * s + 1) * part : (2 * s + 2) * part, :]
+        keep[s, :, :] = jnp.concatenate([jnp.where(core == 0, one, two), weight], axis=0)
+        give[s, :, :] = jnp.concatenate([jnp.where(core == 0, two, one), weight], axis=0)
+
+
+def pair_kernel(keep, given, *refs):
+    outs, both = refs[:-1], refs[-1]
+    side = lax.axis_index("dom") >> 1
+    both[...] = keep[...] + given[...]
+    for s, out in enumerate(outs):
+        out[...] = both[side ^ s]
 
 
 def finish_kernel(width, *refs):
@@ -214,8 +224,7 @@
     width = references.shape[0]
     slots = significant.shape[1]
     step = pixels // ROTS
-    first, second = offsets(blk)
-    pairs = list(zip(first, second))
+    pairs, order = offsets(blk)
     turns = len(pairs)
     total = ROTS * 2 * count
     shape = jax.ShapeDtypeStruct
@@ -227,44 +236,53 @@
 
         return routed(block, dom, blk, move)
 
+    def shared(block, pair):
+        def move(d, b):
+            if pair[0] != 0:
+                return (d, b ^ pair[d & 1])
+            return (d ^ 1, b) if d & 1 else (d ^ 1, b ^ pair[1])
+
+        return routed(block, dom, blk, move)
+
     def over_dom(block, by):
         return routed(block, dom, blk, lambda d, b: (d ^ by, b))
 
-    recv = [over_blk(references, pair) for pair in pairs]
     other = over_dom(particles, 1)
-    live = lax.broadcasted_iota(jnp.int32, (slots, count), 0) < sig_count[None, :]
-    small = jnp.concatenate(
-        [
-            jnp.where(live, significant.T, -1).astype(F32),
-            inv_noise[None, :],
-            jnp.zeros((7, count), F32),
-        ],
-        axis=0,
-    )
-    small_other = over_dom(small, 1)
+    row = lax.broadcasted_iota(jnp.int32, (2 * slots, count), 0)
+    named = jnp.pad(significant.T, ((0, slots), (0, 0)))
+    named = jnp.where(row < sig_count[None, :], named, -1).astype(F32)
+    lists = jnp.where(row < slots, named, inv_noise[None, :])
+    recv = [shared(references, pair) for pair in pairs]
+    lists_other = over_dom(lists, 1)
     (stacked,) = call(stack_kernel, [shape((total, step), BF16)], [particles, other])
     exps, stats = call(
-        functools.partial(forward_kernel, pairs, slots),
+        functools.partial(forward_kernel, pairs),
         [shape((turns * width, total), F32), shape((8, LANES), F32)],
-        [references, *recv, stacked, small, small_other],
+        [*recv, stacked, lists, lists_other],
         [pltpu.VMEM((turns * ROTS * width, step), BF16), pltpu.VMEM((turns * 8, total), F32)],
     )
     stats_other = over_dom(stats, 1)
     rows = ROTS * width
     *sends, own, evidence = call(
-        functools.partial(backward_kernel, turns),
-        [shape((rows + 16, step), BF16)] * turns + [shape((rows + 16, step), F32), shape((1, count), F32)],
+        functools.partial(backward_kernel, pairs),
+        [shape((rows + 8, step), BF16)] * turns + [shape((rows + 8, step), F32), shape((1, count), F32)],
         [exps, stats, stats_other, stacked],
         [pltpu.VMEM((turns * rows, total), BF16)],
     )
-    recv = [over_blk(block, pair) for block, pair in zip(sends, pairs)]
+    recv = [over_blk(sends[t], pairs[t]) for t in order]
+    sides, part = dom // 2, rows // dom + width
+    keep, give = call(
+        functools.partial(gather_kernel, [pairs[t] for t in order], width),
+        [shape((sides, part, step), F32)] * 2,
+        [own, *recv],
+    )
     parts = call(
-        functools.partial(gather_kernel, turns, width),
-        [shape((rows // dom + width, step), F32)] * dom,
-        [own, *recv],
-        [pltpu.VMEM((dom, rows // dom + width, step), F32)],
-    )
-    parts = [parts[0]] + [over_dom(parts[s], s) for s in range(1, dom)]
+        pair_kernel,
+        [shape((part, step), F32)] * sides,
+        [keep, over_dom(give, 1)],
+        [pltpu.VMEM((sides, part, step), F32)],
+    )
+    parts = [parts[0]] + [over_dom(parts[s], 2 * s) for s in range(1, sides)]
     sums, weights = call(
         functools.partial(finish_kernel, width),
         [shape((width, pixels // dom), F32), shape((1, width), F32)],

time: 36.5 us -> 33 us (0.904)
  waiting for transfers between devices: 10.3 us -> 8.89 us
  local copies, waits for them, and re-layouts: 1.89 us -> 1.06 us
  other arithmetic: 1.42 us -> 0.78 us
  starting transfers between devices: 18.9 us -> 18.3 us
    ppermute x14 -> x13, waiting for transfers between devices: 10.3 us -> 8.89 us  [routed(): return lax.ppermute(block, ('dom', 'blk'), pairs)]
    select_n x0 -> x1, other arithmetic: none -> 0.78 us  [body(): lists = jnp.where(row < slots, named, inv_noise[None, :])]
    unnamed x4 -> x2, local copies, waits for them, and re-layouts: 1.81 us -> 1.06 us
    concatenate x1 -> x0, other arithmetic: 0.73 us -> none  [body(): jnp.concatenate([jnp.where(live, significant.T, -1).astype(F32), inv_nois...]
    convert_element_type x1 -> x0, other arithmetic: 0.69 us -> none  [body(): jnp.where(live, significant.T, -1).astype(F32)]
    ppermute x14 -> x13, starting transfers between devices: 18.9 us -> 18.3 us  [routed(): return lax.ppermute(block, ('dom', 'blk'), pairs)]
    pallas_call x5 -> x6, Pallas kernels: 3.08 us -> 3.07 us  [call(): pl.pallas_call(kernel, out_shape=tuple(outs), in_specs=[near] * len(args)...]
  transfers between devices with their start and end apart: 14 -> 13, of which waited for: 6 -> 7; matrix products, arithmetic and copies ran while one was open for 4% -> 2% of each run, Pallas kernels for 0% -> 0%
where the time goes in v2:
time: 33 us; the launch traced here: 32.8 us
  starting transfers between devices  18.3 us (55%)
  waiting for transfers between devices  8.89 us (27%)
  Pallas kernels  3.07 us (9%)
  local copies, waits for them, and re-layouts  1.06 us (3%)
  other arithmetic  0.78 us (2%)
  between operations  0.7 us (2%)
    ppermute x13, starting transfers between devices, routed(): return lax.ppermute(block, ('dom', 'blk'), pairs)  18.3 us
    ppermute x13, waiting for transfers between devices, routed(): return lax.ppermute(block, ('dom', 'blk'), pairs)  8.89 us
    pallas_call x6, Pallas kernels, call(): pl.pallas_call(kernel, out_shape=tuple(outs), in_specs=[near] * len(args)...  3.07 us
    unnamed x2, local copies, waits for them, and re-layouts  1.06 us
    select_n x1, other arithmetic, body(): lists = jnp.where(row < slots, named, inv_noise[None, :])  0.78 us
  transfers between devices with their start and end apart: 13, of which 7 were waited for; matrix products, arithmetic and copies ran while one was open for 2% of the time, Pallas kernels for 0%

profile of v2, /device:TPU:0, one launch (start us, length us, event | category | flops | bytes accessed | tf_op | source)
XLA Modules:
  0.0 32.8 jit_solution(7534644028037261001)
XLA Ops:
  0.6 0.5 %collective-permute-start.4 = (bf16[32,9216]{1,0:T(8,128)(2,1)}, bf16[32,9216]{1,0:T(8,128)(2,1)S(1)}, u32[]{:S(2)}, u32[]{:S(2)}) collective-permute-start(bf16[32,9216]{1,0:T(8,128)(2,1)} %own.1), channel_id=1, source_target_pairs={{0,8},{1,9},{2,10},{3,11},{4,12},{5,13},{6,14},{7,15},{8,0},{9,1},... | collective-permute-start | bytes 1769480 | tf_op jit(solution)/shard_map/ppermute | solution.py:33
  1.1 3.7 %collective-permute-start = (bf16[4,9216]{1,0:T(4,128)(2,1)}, bf16[4,9216]{1,0:T(4,128)(2,1)S(1)}, u32[]{:S(2)}, u32[]{:S(2)}) collective-permute-start(bf16[4,9216]{1,0:T(4,128)(2,1)} %param.6), channel_id=1, source_target_pairs={{0,4},{1,5},{2,6},{3,7},{4,0},{5,1},{6,2},{7,3},{8,15},{9,14},{10,... | collective-permute-start | bytes 221192 | tf_op jit(solution)/shard_map/ppermute | solution.py:33
  4.8 1.3 %collective-permute-start.1 = (bf16[4,9216]{1,0:T(4,128)(2,1)}, bf16[4,9216]{1,0:T(4,128)(2,1)S(1)}, u32[]{:S(2)}, u32[]{:S(2)}) collective-permute-start(bf16[4,9216]{1,0:T(4,128)(2,1)} %param.6), channel_id=1, source_target_pairs={{0,5},{1,4},{2,7},{3,6},{4,1},{5,0},{6,3},{7,2},{8,11},{9,10},{10,... | collective-permute-start | bytes 221192 | tf_op jit(solution)/shard_map/ppermute | solution.py:33
  6.1 3.6 %collective-permute-start.2 = (bf16[4,9216]{1,0:T(4,128)(2,1)}, bf16[4,9216]{1,0:T(4,128)(2,1)S(1)}, u32[]{:S(2)}, u32[]{:S(2)}) collective-permute-start(bf16[4,9216]{1,0:T(4,128)(2,1)} %param.6), channel_id=1, source_target_pairs={{0,6},{1,7},{2,4},{3,5},{4,2},{5,3},{6,0},{7,1},{8,10},{9,11},{10,... | collective-permute-start | bytes 221192 | tf_op jit(solution)/shard_map/ppermute | solution.py:33
  9.7 0.0 collective-permute-start.3
  9.7 0.8 %convert_select_fusion.refs_5_ = f32[16,32]{1,0:T(8,128)S(1)} fusion(s32[8,32]{1,0:T(8,128)} %bitcast.3, f32[32]{0:T(128)} %param.7, s32[32]{0:T(128)} %param.9, pred[16]{0:T(512)(128)(4,1)S(1)} %iota_compare_fusion.1), kind=kLoop, calls=%fused_computation | loop fusion | flops 2048 | bytes 3344 | tf_op jit(solution)/shard_map/jit(_where)/select_n | solution.py:254
  10.5 0.0 collective-permute-done.4.other
  10.5 0.5 %collective-permute-start.5 = (f32[16,32]{1,0:T(8,128)S(1)}, f32[16,32]{1,0:T(8,128)S(1)}, u32[]{:S(2)}, u32[]{:S(2)}) collective-permute-start(f32[16,32]{1,0:T(8,128)S(1)} %convert_select_fusion.refs_5_), channel_id=1, source_target_pairs={{0,8},{1,9},{2,10},{3,11},{4,12},{5,13},{6,14},{7,15},{8,0},{9,1},... | collective-permute-start | bytes 6152 | tf_op jit(solution)/shard_map/ppermute | solution.py:33
  11.0 1.1 %copy-done = bf16[32,9216]{1,0:T(8,128)(2,1)S(1)} copy-done((bf16[32,9216]{1,0:T(8,128)(2,1)S(1)}, bf16[32,9216]{1,0:T(8,128)(2,1)}, u32[]{:S(2)}) %copy-start) | copy-done | bytes 589848
  12.1 0.1 shard_map.76.refs_4_.refs_3_
  12.2 0.0 collective-permute-done.refs_0_
  12.2 0.0 collective-permute-done.1.refs_1_
  12.2 0.9 %collective-permute-done.2.refs_2_ = bf16[4,9216]{1,0:T(4,128)(2,1)S(1)} collective-permute-done((bf16[4,9216]{1,0:T(4,128)(2,1)}, bf16[4,9216]{1,0:T(4,128)(2,1)S(1)}, u32[]{:S(2)}, u32[]{:S(2)}) %collective-permute-start.2) | collective-permute-done | bytes 73760 | tf_op jit(solution)/shard_map/ppermute | solution.py:33
  13.1 0.0 collective-permute-done.3.refs_3_
  13.1 1.2 %shard_map.77 = (f32[16,2304]{1,0:T(8,128)S(1)}, f32[8,128]{1,0:T(8,128)S(1)}) custom-call(bf16[4,9216]{1,0:T(4,128)(2,1)S(1)} %collective-permute-done.refs_0_, bf16[4,9216]{1,0:T(4,128)(2,1)S(1)} %collective-permute-done.1.refs_1_, bf16[4,9216]{1,0:T(4,128)(2,1)S(1)} %collective-permute-done.2.refs_2_, bf16[4,9216]{1,0:T(4,128)(2,1)S(1)} %collective-permute-done.3.refs_3_, ...), custom_call_target="tpu_custom_call" | custom-call | flops 1000000 | bytes 1630208 | tf_op jit(solution)/shard_map/pallas_call | solution.py:39
  14.4 0.0 collective-permute-start.6
  14.4 1.2 %collective-permute-done.6.refs_2_ = f32[8,128]{1,0:T(8,128)S(1)} collective-permute-done((f32[8,128]{1,0:T(8,128)S(1)}, f32[8,128]{1,0:T(8,128)S(1)}, u32[]{:S(2)}, u32[]{:S(2)}) %collective-permute-start.6) | collective-permute-done | bytes 4128 | tf_op jit(solution)/shard_map/ppermute | solution.py:33
  15.5 1.0 %shard_map.78 = (bf16[152,256]{1,0:T(8,128)(2,1)S(1)}, bf16[152,256]{1,0:T(8,128)(2,1)S(1)}, bf16[152,256]{1,0:T(8,128)(2,1)S(1)}, bf16[152,256]{1,0:T(8,128)(2,...) custom-call(f32[16,2304]{1,0:T(8,128)S(1)} %get-tuple-element.17.refs_0_, f32[8,128]{1,0:T(8,128)S(1)} %get-tuple-element.18.refs_1_, ...), custom_call_target="tpu_custom_call" | custom-call | flops 1000000 | bytes 1802368 | tf_op jit(solution)/shard_map/pallas_call | solution.py:39
  16.5 2.2 %collective-permute-start.10 = (bf16[152,256]{1,0:T(8,128)(2,1)S(1)}, bf16[152,256]{1,0:T(8,128)(2,1)S(1)}, u32[]{:S(2)}, u32[]{:S(2)}) collective-permute-start(bf16[152,256]{1,0:T(8,128)(2,1)S(1)} %get-tuple-element.23), channel_id=1, source_target_pairs={{0,4},{1,5},{2,6},{3,7},{4,0},{5,1},{6,2},{7,3},{8,15},{9,14},{10,... | collective-permute-start | bytes 233480 | tf_op jit(solution)/shard_map/ppermute | solution.py:33
  18.8 0.9 %collective-permute-start.7 = (bf16[152,256]{1,0:T(8,128)(2,1)S(1)}, bf16[152,256]{1,0:T(8,128)(2,1)S(1)}, u32[]{:S(2)}, u32[]{:S(2)}) collective-permute-start(bf16[152,256]{1,0:T(8,128)(2,1)S(1)} %get-tuple-element.20), channel_id=1, source_target_pairs={{0,5},{1,4},{2,7},{3,6},{4,1},{5,0},{6,3},{7,2},{8,11},{9,10},{10,... | collective-permute-start | bytes 233480 | tf_op jit(solution)/shard_map/ppermute | solution.py:33
  19.6 3.0 %collective-permute-start.8 = (bf16[152,256]{1,0:T(8,128)(2,1)S(1)}, bf16[152,256]{1,0:T(8,128)(2,1)S(1)}, u32[]{:S(2)}, u32[]{:S(2)}) collective-permute-start(bf16[152,256]{1,0:T(8,128)(2,1)S(1)} %get-tuple-element.21), channel_id=1, source_target_pairs={{0,6},{1,7},{2,4},{3,5},{4,2},{5,3},{6,0},{7,1},{8,10},{9,11},{10,... | collective-permute-start | bytes 233480 | tf_op jit(solution)/shard_map/ppermute | solution.py:33
  22.6 0.7 %collective-permute-start.9 = (bf16[152,256]{1,0:T(8,128)(2,1)S(1)}, bf16[152,256]{1,0:T(8,128)(2,1)S(1)}, u32[]{:S(2)}, u32[]{:S(2)}) collective-permute-start(bf16[152,256]{1,0:T(8,128)(2,1)S(1)} %get-tuple-element.22), channel_id=1, source_target_pairs={{8,9},{9,8},{10,11},{11,10},{12,13},{13,12},{14,15},{15,14},{24,25... | collective-permute-start | bytes 233480 | tf_op jit(solution)/shard_map/ppermute | solution.py:33
  23.3 0.4 %collective-permute-done.10.refs_4_ = bf16[152,256]{1,0:T(8,128)(2,1)S(1)} collective-permute-done((bf16[152,256]{1,0:T(8,128)(2,1)S(1)}, bf16[152,256]{1,0:T(8,128)(2,1)S(1)}, u32[]{:S(2)}, u32[]{:S(2)}) %collective-permute-start.10) | collective-permute-done | bytes 77856 | tf_op jit(solution)/shard_map/ppermute | solution.py:33
  23.6 1.3 %collective-permute-done.7.refs_1_ = bf16[152,256]{1,0:T(8,128)(2,1)S(1)} collective-permute-done((bf16[152,256]{1,0:T(8,128)(2,1)S(1)}, bf16[152,256]{1,0:T(8,128)(2,1)S(1)}, u32[]{:S(2)}, u32[]{:S(2)}) %collective-permute-start.7) | collective-permute-done | bytes 77856 | tf_op jit(solution)/shard_map/ppermute | solution.py:33
  25.0 1.7 %collective-permute-done.8.refs_2_ = bf16[152,256]{1,0:T(8,128)(2,1)S(1)} collective-permute-done((bf16[152,256]{1,0:T(8,128)(2,1)S(1)}, bf16[152,256]{1,0:T(8,128)(2,1)S(1)}, u32[]{:S(2)}, u32[]{:S(2)}) %collective-permute-start.8) | collective-permute-done | bytes 77856 | tf_op jit(solution)/shard_map/ppermute | solution.py:33
  26.6 0.0 collective-permute-done.9.refs_3_
  26.6 0.1 shard_map.79
  26.8 0.4 %collective-permute-start.11 = (f32[2,40,256]{2,1,0:T(8,128)S(1)}, f32[2,40,256]{2,1,0:T(8,128)S(1)}, u32[]{:S(2)}, u32[]{:S(2)}) collective-permute-start(f32[2,40,256]{2,1,0:T(8,128)S(1)} %get-tuple-element.25), channel_id=1, source_target_pairs={{0,8},{1,9},{2,10},{3,11},{4,12},{5,13},{6,14},{7,15},{8,0},{9,1},... | collective-permute-start | bytes 245768 | tf_op jit(solution)/shard_map/ppermute | solution.py:33
  27.1 0.9 %collective-permute-done.11.given = f32[2,40,256]{2,1,0:T(8,128)S(1)} collective-permute-done((f32[2,40,256]{2,1,0:T(8,128)S(1)}, f32[2,40,256]{2,1,0:T(8,128)S(1)}, u32[]{:S(2)}, u32[]{:S(2)}) %collective-permute-start.11) | collective-permute-done | bytes 81952 | tf_op jit(solution)/shard_map/ppermute | solution.py:33
  28.1 1.6 %collective-permute-start.12 = (f32[40,256]{1,0:T(8,128)S(1)}, f32[40,256]{1,0:T(8,128)S(1)}, u32[]{:S(2)}, u32[]{:S(2)}) collective-permute-start(f32[40,256]{1,0:T(8,128)S(1)} %get-tuple-element.27), channel_id=1, source_target_pairs={{0,16},{1,17},{2,18},{3,19},{4,20},{5,21},{6,22},{7,23},{8,24},{9,... | collective-permute-start | bytes 122888 | tf_op jit(solution)/shard_map/ppermute | solution.py:33
  29.7 2.5 %collective-permute-done.12.refs_1_ = f32[40,256]{1,0:T(8,128)S(1)} collective-permute-done((f32[40,256]{1,0:T(8,128)S(1)}, f32[40,256]{1,0:T(8,128)S(1)}, u32[]{:S(2)}, u32[]{:S(2)}) %collective-permute-start.12) | collective-permute-done | bytes 40992 | tf_op jit(solution)/shard_map/ppermute | solution.py:33
  32.2 0.6 %shard_map.81 = (f32[4,2304]{1,0:T(4,128)}, f32[1,4]{1,0:T(1,128)}) custom-call(f32[40,256]{1,0:T(8,128)S(1)} %get-tuple-element.26.refs_0_, f32[40,256]{1,0:T(8,128)S(1)} %collective-permute-done.12.refs_1_), custom_call_target="tpu_custom_call" | custom-call | flops 1000000 | bytes 118800 | tf_op jit(solution)/shard_map/pallas_call | solution.py:39
  (4 shorter events, 0.0 us)
Async XLA Ops:
  0.6 9.8 %collective-permute-start.4 = (bf16[32,9216]{1,0:T(8,128)(2,1)}, bf16[32,9216]{1,0:T(8,128)(2,1)S(1)}, u32[]{:S(2)}, u32[]{:S(2)}) collective-permute-start(bf16[32,9216]{1,0:T(8,128)(2,1)} %own.1), channel_id=1, source_target_pairs={{0,8},{1,9},{2,10},{3,11},{4,12},{5,13},{6,14},{7,15},{8,0},{9,1},... | collective-permute-start | bytes 1769480 | tf_op jit(solution)/shard_map/ppermute | solution.py:33
  1.1 11.0 %collective-permute-start = (bf16[4,9216]{1,0:T(4,128)(2,1)}, bf16[4,9216]{1,0:T(4,128)(2,1)S(1)}, u32[]{:S(2)}, u32[]{:S(2)}) collective-permute-start(bf16[4,9216]{1,0:T(4,128)(2,1)} %param.6), channel_id=1, source_target_pairs={{0,4},{1,5},{2,6},{3,7},{4,0},{5,1},{6,2},{7,3},{8,15},{9,14},{10,... | collective-permute-start | bytes 221192 | tf_op jit(solution)/shard_map/ppermute | solution.py:33
  4.8 7.4 %collective-permute-start.1 = (bf16[4,9216]{1,0:T(4,128)(2,1)}, bf16[4,9216]{1,0:T(4,128)(2,1)S(1)}, u32[]{:S(2)}, u32[]{:S(2)}) collective-permute-start(bf16[4,9216]{1,0:T(4,128)(2,1)} %param.6), channel_id=1, source_target_pairs={{0,5},{1,4},{2,7},{3,6},{4,1},{5,0},{6,3},{7,2},{8,11},{9,10},{10,... | collective-permute-start | bytes 221192 | tf_op jit(solution)/shard_map/ppermute | solution.py:33
  6.1 7.0 %collective-permute-start.2 = (bf16[4,9216]{1,0:T(4,128)(2,1)}, bf16[4,9216]{1,0:T(4,128)(2,1)S(1)}, u32[]{:S(2)}, u32[]{:S(2)}) collective-permute-start(bf16[4,9216]{1,0:T(4,128)(2,1)} %param.6), channel_id=1, source_target_pairs={{0,6},{1,7},{2,4},{3,5},{4,2},{5,3},{6,0},{7,1},{8,10},{9,11},{10,... | collective-permute-start | bytes 221192 | tf_op jit(solution)/shard_map/ppermute | solution.py:33
  9.7 3.4 %collective-permute-start.3 = (bf16[4,9216]{1,0:T(4,128)(2,1)}, bf16[4,9216]{1,0:T(4,128)(2,1)S(1)}, u32[]{:S(2)}, u32[]{:S(2)}) collective-permute-start(bf16[4,9216]{1,0:T(4,128)(2,1)} %param.6), channel_id=1, source_target_pairs={{0,9},{1,8},{2,11},{3,10},{4,13},{5,12},{6,15},{7,14},{8,0},{9,1},... | collective-permute-start | bytes 221192 | tf_op jit(solution)/shard_map/ppermute | solution.py:33
  10.5 1.7 %collective-permute-start.5 = (f32[16,32]{1,0:T(8,128)S(1)}, f32[16,32]{1,0:T(8,128)S(1)}, u32[]{:S(2)}, u32[]{:S(2)}) collective-permute-start(f32[16,32]{1,0:T(8,128)S(1)} %convert_select_fusion.refs_5_), channel_id=1, source_target_pairs={{0,8},{1,9},{2,10},{3,11},{4,12},{5,13},{6,14},{7,15},{8,0},{9,1},... | collective-permute-start | bytes 6152 | tf_op jit(solution)/shard_map/ppermute | solution.py:33
  11.0 1.1 %copy-start = (bf16[32,9216]{1,0:T(8,128)(2,1)S(1)}, bf16[32,9216]{1,0:T(8,128)(2,1)}, u32[]{:S(2)}) copy-start(bf16[32,9216]{1,0:T(8,128)(2,1)} %own.1) | copy-start | bytes 1769476
  14.4 1.2 %collective-permute-start.6 = (f32[8,128]{1,0:T(8,128)S(1)}, f32[8,128]{1,0:T(8,128)S(1)}, u32[]{:S(2)}, u32[]{:S(2)}) collective-permute-start(f32[8,128]{1,0:T(8,128)S(1)} %get-tuple-element.18.refs_1_), channel_id=1, source_target_pairs={{0,8},{1,9},{2,10},{3,11},{4,12},{5,13},{6,14},{7,15},{8,0},{9,1},... | collective-permute-start | bytes 12296 | tf_op jit(solution)/shard_map/ppermute | solution.py:33
  16.5 7.1 %collective-permute-start.10 = (bf16[152,256]{1,0:T(8,128)(2,1)S(1)}, bf16[152,256]{1,0:T(8,128)(2,1)S(1)}, u32[]{:S(2)}, u32[]{:S(2)}) collective-permute-start(bf16[152,256]{1,0:T(8,128)(2,1)S(1)} %get-tuple-element.23), channel_id=1, source_target_pairs={{0,4},{1,5},{2,6},{3,7},{4,0},{5,1},{6,2},{7,3},{8,15},{9,14},{10,... | collective-permute-start | bytes 233480 | tf_op jit(solution)/shard_map/ppermute | solution.py:33
  18.8 6.2 %collective-permute-start.7 = (bf16[152,256]{1,0:T(8,128)(2,1)S(1)}, bf16[152,256]{1,0:T(8,128)(2,1)S(1)}, u32[]{:S(2)}, u32[]{:S(2)}) collective-permute-start(bf16[152,256]{1,0:T(8,128)(2,1)S(1)} %get-tuple-element.20), channel_id=1, source_target_pairs={{0,5},{1,4},{2,7},{3,6},{4,1},{5,0},{6,3},{7,2},{8,11},{9,10},{10,... | collective-permute-start | bytes 233480 | tf_op jit(solution)/shard_map/ppermute | solution.py:33
  19.6 7.0 %collective-permute-start.8 = (bf16[152,256]{1,0:T(8,128)(2,1)S(1)}, bf16[152,256]{1,0:T(8,128)(2,1)S(1)}, u32[]{:S(2)}, u32[]{:S(2)}) collective-permute-start(bf16[152,256]{1,0:T(8,128)(2,1)S(1)} %get-tuple-element.21), channel_id=1, source_target_pairs={{0,6},{1,7},{2,4},{3,5},{4,2},{5,3},{6,0},{7,1},{8,10},{9,11},{10,... | collective-permute-start | bytes 233480 | tf_op jit(solution)/shard_map/ppermute | solution.py:33
  22.6 4.1 %collective-permute-start.9 = (bf16[152,256]{1,0:T(8,128)(2,1)S(1)}, bf16[152,256]{1,0:T(8,128)(2,1)S(1)}, u32[]{:S(2)}, u32[]{:S(2)}) collective-permute-start(bf16[152,256]{1,0:T(8,128)(2,1)S(1)} %get-tuple-element.22), channel_id=1, source_target_pairs={{8,9},{9,8},{10,11},{11,10},{12,13},{13,12},{14,15},{15,14},{24,25... | collective-permute-start | bytes 233480 | tf_op jit(solution)/shard_map/ppermute | solution.py:33
  26.8 1.3 %collective-permute-start.11 = (f32[2,40,256]{2,1,0:T(8,128)S(1)}, f32[2,40,256]{2,1,0:T(8,128)S(1)}, u32[]{:S(2)}, u32[]{:S(2)}) collective-permute-start(f32[2,40,256]{2,1,0:T(8,128)S(1)} %get-tuple-element.25), channel_id=1, source_target_pairs={{0,8},{1,9},{2,10},{3,11},{4,12},{5,13},{6,14},{7,15},{8,0},{9,1},... | collective-permute-start | bytes 245768 | tf_op jit(solution)/shard_map/ppermute | solution.py:33
  28.1 4.1 %collective-permute-start.12 = (f32[40,256]{1,0:T(8,128)S(1)}, f32[40,256]{1,0:T(8,128)S(1)}, u32[]{:S(2)}, u32[]{:S(2)}) collective-permute-start(f32[40,256]{1,0:T(8,128)S(1)} %get-tuple-element.27), channel_id=1, source_target_pairs={{0,16},{1,17},{2,18},{3,19},{4,20},{5,21},{6,22},{7,23},{8,24},{9,... | collective-permute-start | bytes 122888 | tf_op jit(solution)/shard_map/ppermute | solution.py:33

commit v3 on v2

--- a/solution.py
+++ b/solution.py
@@ -64,31 +64,24 @@
     return jnp.concatenate([own, other, own, other], axis=1)
 
 
-def forward_kernel(pairs, *refs):
-    turns = len(pairs)
-    recv = refs[:turns]
-    stacked, lists_own, lists_other, exps, stats, tiles, acc = refs[turns:]
-    core = lax.axis_index("dom") & 1
-    spot = lax.axis_index("blk")
+def correlate(recv, stacked, tiles):
     width, pixels = recv[0].shape
-    slots = lists_own.shape[0] // 2
-    lists = lanes_of(lists_own[...], lists_other[...])
     step = pixels // ROTS
     total = stacked.shape[0]
     columns = total // LANES
     rows = ROTS * width
     norms = []
-    for t in range(turns):
-        block = recv[t][...].astype(F32)
-        norms.append(jnp.sum(block * block, axis=1, keepdims=True))
+    for t, ref in enumerate(recv):
+        block = ref[...].astype(F32)
+        norms.append(0.5 * jnp.sum(block * block, axis=1, keepdims=True))
         for u in range(ROTS // 4):
             tile = jnp.concatenate([block[:, (4 * u + a) * step : (4 * u + a + 1) * step] for a in range(4)], axis=0)
             tiles[t * rows + 16 * u : t * rows + 16 * (u + 1), :] = tile.astype(BF16)
-    acc[...] = jnp.zeros_like(acc)
+    sums = [[None] * columns for _ in recv]
     for n in range(columns // 2):
         weights = stacked[n * 256 : (n + 1) * 256, :]
         got = lax.dot_general(tiles[...], weights, (((1,), (1,)), ((), ())), preferred_element_type=F32)
-        for t in range(turns):
+        for t, held in enumerate(sums):
             for m in range(-1, columns):
                 part = None
                 if m >= 0:
@@ -96,14 +89,35 @@
                 if m + 1 < columns:
                     extra = got[t * rows + 8 * m + 8 : t * rows + 8 * m + 16, LANES:]
                     part = extra if part is None else part + extra
-                place = ((2 * n - m) % columns) * LANES
-                acc[8 * t : 8 * t + 8, place : place + LANES] += part
+                place = (2 * n - m) % columns
+                held[place] = part if held[place] is None else held[place] + part
     corr = []
-    for t in range(turns):
-        odd = pltpu.roll(acc[8 * t + 4 : 8 * t + 8, :], total - 64, 1)
-        corr.append(acc[8 * t : 8 * t + 4, :] + odd)
-    corr = jnp.concatenate(corr, axis=0)
-    norm = jnp.concatenate(norms, axis=0)
+    for held in sums:
+        whole = jnp.concatenate(held, axis=1)
+        corr.append(whole[:4, :] + pltpu.roll(whole, total - 64, 1)[4:, :])
+    return jnp.concatenate(corr, axis=0), jnp.concatenate(norms, axis=0)
+
+
+def early_kernel(*refs):
+    recv, (stacked, corr, norm, tiles) = refs[:-4], refs[-4:]
+    value, norms = correlate(recv, stacked, tiles)
+    corr[...] = value
+    norm[...] = jnp.broadcast_to(norms, norm.shape)
+
+
+def forward_kernel(pairs, *refs):
+    recv, (stacked, lists_own, lists_other) = refs[:-9], refs[-9:-6]
+    early, early_norm, exps, stats, tiles, corr = refs[-6:]
+    core = lax.axis_index("dom") & 1
+    spot = lax.axis_index("blk")
+    width = recv[0].shape[0]
+    slots = lists_own.shape[0] // 2
+    columns = stacked.shape[0] // LANES
+    late, late_norm = correlate(recv, stacked, tiles)
+    corr[: early.shape[0], :] = early[...]
+    corr[early.shape[0] :, :] = late
+    norm = jnp.concatenate([early_norm[...], jnp.broadcast_to(late_norm, (late_norm.shape[0], LANES))], axis=0)
+    lists = lanes_of(lists_own[...], lists_other[...])
     inverse = lists[slots : slots + 1, :]
     ids = jnp.concatenate(
         [
@@ -115,7 +129,7 @@
     mask = lists[0:1, :] == ids
     for s in range(1, slots):
         mask = mask | (lists[s : s + 1, :] == ids)
-    scores = [inverse * (corr[:, c * LANES : (c + 1) * LANES] - 0.5 * norm) for c in range(columns)]
+    scores = [inverse * (corr[:, c * LANES : (c + 1) * LANES] - norm) for c in range(columns)]
     peak = jnp.full(ids.shape, LOW, F32)
     for score in scores:
         peak = jnp.maximum(peak, score)
@@ -132,38 +146,38 @@
 
 
 def backward_kernel(pairs, *refs):
-    turns = len(pairs)
+    taken = range(len(pairs))
     exps, mine, theirs, stacked = refs[:4]
-    sends, (own, evidence, left) = refs[4 : 4 + turns], refs[4 + turns :]
+    sends, (own, evidence, left) = refs[4:-3], refs[-3:]
     total = stacked.shape[0]
     columns = total // LANES
-    width = exps.shape[0] // turns
+    width = exps.shape[0] // len(pairs)
     rows = ROTS * width
-    extra_rows = own.shape[0] - rows
+    extra_rows, step = sends[0].shape[0] - rows, sends[0].shape[1]
     peak, mass = mine[0:1, :], mine[1:2, :]
     peak_far, mass_far = pltpu.roll(theirs[0:1, :], 32, 1), pltpu.roll(theirs[1:2, :], 32, 1)
     top = jnp.maximum(peak, peak_far)
     share = jnp.exp(peak - top)
     whole = mass * share + mass_far * jnp.exp(peak_far - top)
+    factor = share / whole
     evidence[...] = (top + jnp.log(whole))[:, : evidence.shape[1]]
-    factor = share / whole
-    post = jnp.concatenate([exps[:, c * LANES : (c + 1) * LANES] * factor for c in range(columns)], axis=1)
-    weight = jnp.sum(post, axis=1, keepdims=True)
-    turned = pltpu.roll(post, 64, 1)
-    for t in range(turns):
-        two = jnp.concatenate([post[width * t : width * (t + 1), :], turned[width * t : width * (t + 1), :]], axis=0)
+    weights = []
+    for n, t in enumerate(taken):
+        post = jnp.concatenate(
+            [exps[width * t : width * (t + 1), c * LANES : (c + 1) * LANES] * factor for c in range(columns)], axis=1
+        )
+        weights.append(jnp.sum(post, axis=1, keepdims=True))
+        two = jnp.concatenate([post, pltpu.roll(post, 64, 1)], axis=0)
         four = jnp.concatenate([two, pltpu.roll(two, 128, 1)], axis=0).astype(BF16)
         for u in range(ROTS // 4):
             cut = total - 256 * u
             rotated = four if u == 0 else jnp.concatenate([four[:, cut:], four[:, :cut]], axis=1)
-            left[t * rows + 16 * u : t * rows + 16 * (u + 1), :] = rotated
+            left[n * rows + 16 * u : n * rows + 16 * (u + 1), :] = rotated
     result = jnp.dot(left[...], stacked[...], preferred_element_type=F32)
-    lane = lax.broadcasted_iota(jnp.int32, (extra_rows, own.shape[1]), 1)
-    row = lax.broadcasted_iota(jnp.int32, (extra_rows, own.shape[1]), 0)
-    for t in range(turns):
-        piece = weight[width * t : width * (t + 1), :]
-        piece = jnp.concatenate([piece, jnp.zeros((extra_rows - width, 1), F32)], axis=0)
-        block = result[t * rows : (t + 1) * rows, :]
+    lane = lax.broadcasted_iota(jnp.int32, (extra_rows, step), 1)
+    for n, t in enumerate(taken):
+        piece = jnp.concatenate([weights[n], jnp.zeros((extra_rows - width, 1), F32)], axis=0)
+        block = result[n * rows : (n + 1) * rows, :]
         high = piece.astype(BF16).astype(F32)
         middle = (piece - high).astype(BF16).astype(F32)
         low = piece - high - middle
@@ -171,7 +185,7 @@
             own[:rows, :] = block
             own[rows:, :] = jnp.where(lane == 0, piece, 0.0)
         tail = jnp.where(lane == 0, high, jnp.where(lane == 1, middle, jnp.where(lane == 2, low, 0.0)))
-        sends[t][...] = jnp.concatenate([block, tail], axis=0).astype(BF16)
+        sends[n][...] = jnp.concatenate([block, tail], axis=0).astype(BF16)
 
 
 def gather_kernel(pairs, width, *refs):
@@ -255,19 +269,34 @@
     recv = [shared(references, pair) for pair in pairs]
     lists_other = over_dom(lists, 1)
     (stacked,) = call(stack_kernel, [shape((total, step), BF16)], [particles, other])
+    rows = ROTS * width
+
+    def buffers(blocks):
+        return [pltpu.VMEM((blocks * rows, step), BF16)]
+
+    early = turns // 2
+    corr, norm = call(
+        early_kernel,
+        [shape((early * width, total), F32), shape((early * width, LANES), F32)],
+        [*recv[:early], stacked],
+        buffers(early),
+        flops=2 * early * rows * step * total,
+    )
     exps, stats = call(
         functools.partial(forward_kernel, pairs),
         [shape((turns * width, total), F32), shape((8, LANES), F32)],
-        [*recv, stacked, lists, lists_other],
-        [pltpu.VMEM((turns * ROTS * width, step), BF16), pltpu.VMEM((turns * 8, total), F32)],
+        [*recv[early:], stacked, lists, lists_other, corr, norm],
+        buffers(turns - early) + [pltpu.VMEM((turns * width, total), F32)],
+        flops=2 * (turns - early) * rows * step * total,
     )
     stats_other = over_dom(stats, 1)
-    rows = ROTS * width
+    message = shape((rows + 8, step), BF16)
     *sends, own, evidence = call(
         functools.partial(backward_kernel, pairs),
-        [shape((rows + 8, step), BF16)] * turns + [shape((rows + 8, step), F32), shape((1, count), F32)],
+        [message] * turns + [shape((rows + 8, step), F32), shape((1, count), F32)],
         [exps, stats, stats_other, stacked],
         [pltpu.VMEM((turns * rows, total), BF16)],
+        flops=2 * turns * rows * step * total,
     )
     recv = [over_blk(sends[t], pairs[t]) for t in order]
     sides, part = dom // 2, rows // dom + width

time: 33 us -> 32.6 us (0.988)
  waiting for transfers between devices: 8.89 us -> 8.27 us
    ppermute x13, waiting for transfers between devices: 8.89 us -> 8.27 us  [routed(): return lax.ppermute(block, ('dom', 'blk'), pairs)]
    pallas_call x6 -> x7, Pallas kernels: 3.07 us -> 3.32 us  [call(): pl.pallas_call(kernel, out_shape=tuple(outs), in_specs=[near] * len(args)...]
  transfers between devices with their start and end apart: 13 -> 13, of which waited for: 7 -> 7; matrix products, arithmetic and copies ran while one was open for 2% -> 2% of each run, Pallas kernels for 0% -> 2%
where the time goes in v3:
time: 32.6 us; the launch traced here: 32.4 us
  starting transfers between devices  18.3 us (56%)
  waiting for transfers between devices  8.27 us (25%)
  Pallas kernels  3.32 us (10%)
  local copies, waits for them, and re-layouts  1.06 us (3%)
  other arithmetic  0.78 us (2%)
  between operations  0.7 us (2%)
    ppermute x13, starting transfers between devices, routed(): return lax.ppermute(block, ('dom', 'blk'), pairs)  18.3 us
    ppermute x13, waiting for transfers between devices, routed(): return lax.ppermute(block, ('dom', 'blk'), pairs)  8.27 us
    pallas_call x7, Pallas kernels, call(): pl.pallas_call(kernel, out_shape=tuple(outs), in_specs=[near] * len(args)...  3.32 us
    unnamed x2, local copies, waits for them, and re-layouts  1.06 us
    select_n x1, other arithmetic, body(): lists = jnp.where(row < slots, named, inv_noise[None, :])  0.78 us
  transfers between devices with their start and end apart: 13, of which 7 were waited for; matrix products, arithmetic and copies ran while one was open for 2% of the time, Pallas kernels for 2%

profile of v3, /device:TPU:0, one launch (start us, length us, event | category | flops | bytes accessed | tf_op | source)
XLA Modules:
  0.0 32.4 jit_solution(18151865904265562559)
XLA Ops:
  0.6 0.5 %collective-permute-start.2 = (bf16[32,9216]{1,0:T(8,128)(2,1)}, bf16[32,9216]{1,0:T(8,128)(2,1)S(1)}, u32[]{:S(2)}, u32[]{:S(2)}) collective-permute-start(bf16[32,9216]{1,0:T(8,128)(2,1)} %own.1), channel_id=1, source_target_pairs={{0,8},{1,9},{2,10},{3,11},{4,12},{5,13},{6,14},{7,15},{8,0},{9,1},... | collective-permute-start | bytes 1769480 | tf_op jit(solution)/shard_map/ppermute | solution.py:33
  1.1 3.7 %collective-permute-start.4 = (bf16[4,9216]{1,0:T(4,128)(2,1)}, bf16[4,9216]{1,0:T(4,128)(2,1)S(1)}, u32[]{:S(2)}, u32[]{:S(2)}) collective-permute-start(bf16[4,9216]{1,0:T(4,128)(2,1)} %param.6), channel_id=1, source_target_pairs={{0,4},{1,5},{2,6},{3,7},{4,0},{5,1},{6,2},{7,3},{8,15},{9,14},{10,... | collective-permute-start | bytes 221192 | tf_op jit(solution)/shard_map/ppermute | solution.py:33
  4.8 1.3 %collective-permute-start.5 = (bf16[4,9216]{1,0:T(4,128)(2,1)}, bf16[4,9216]{1,0:T(4,128)(2,1)S(1)}, u32[]{:S(2)}, u32[]{:S(2)}) collective-permute-start(bf16[4,9216]{1,0:T(4,128)(2,1)} %param.6), channel_id=1, source_target_pairs={{0,5},{1,4},{2,7},{3,6},{4,1},{5,0},{6,3},{7,2},{8,11},{9,10},{10,... | collective-permute-start | bytes 221192 | tf_op jit(solution)/shard_map/ppermute | solution.py:33
  6.1 3.6 %collective-permute-start = (bf16[4,9216]{1,0:T(4,128)(2,1)}, bf16[4,9216]{1,0:T(4,128)(2,1)S(1)}, u32[]{:S(2)}, u32[]{:S(2)}) collective-permute-start(bf16[4,9216]{1,0:T(4,128)(2,1)} %param.6), channel_id=1, source_target_pairs={{0,6},{1,7},{2,4},{3,5},{4,2},{5,3},{6,0},{7,1},{8,10},{9,11},{10,... | collective-permute-start | bytes 221192 | tf_op jit(solution)/shard_map/ppermute | solution.py:33
  9.7 0.0 collective-permute-start.1
  9.7 0.8 %convert_select_fusion.refs_3_ = f32[16,32]{1,0:T(8,128)S(1)} fusion(s32[8,32]{1,0:T(8,128)} %bitcast.3, f32[32]{0:T(128)} %param.7, s32[32]{0:T(128)} %param.9, pred[16]{0:T(512)(128)(4,1)S(1)} %iota_compare_fusion.1), kind=kLoop, calls=%fused_computation | loop fusion | flops 2048 | bytes 3344 | tf_op jit(solution)/shard_map/jit(_where)/select_n | solution.py:268
  10.5 0.0 collective-permute-done.2.other
  10.5 0.5 %collective-permute-start.3 = (f32[16,32]{1,0:T(8,128)S(1)}, f32[16,32]{1,0:T(8,128)S(1)}, u32[]{:S(2)}, u32[]{:S(2)}) collective-permute-start(f32[16,32]{1,0:T(8,128)S(1)} %convert_select_fusion.refs_3_), channel_id=1, source_target_pairs={{0,8},{1,9},{2,10},{3,11},{4,12},{5,13},{6,14},{7,15},{8,0},{9,1},... | collective-permute-start | bytes 6152 | tf_op jit(solution)/shard_map/ppermute | solution.py:33
  11.0 1.1 %copy-done = bf16[32,9216]{1,0:T(8,128)(2,1)S(1)} copy-done((bf16[32,9216]{1,0:T(8,128)(2,1)S(1)}, bf16[32,9216]{1,0:T(8,128)(2,1)}, u32[]{:S(2)}) %copy-start) | copy-done | bytes 589848
  12.1 0.1 shard_map.76.refs_2_.refs_3_
  12.2 0.0 collective-permute-done.4.refs_0_
  12.2 0.6 %shard_map.77 = (f32[8,2304]{1,0:T(8,128)S(1)}, f32[8,128]{1,0:T(8,128)S(1)}) custom-call(bf16[4,9216]{1,0:T(4,128)(2,1)S(1)} %collective-permute-done.4.refs_0_, bf16[4,9216]{1,0:T(4,128)(2,1)S(1)} %collective-permute-done.5.refs_1_, bf16[2304,256]{1,0:T(8,128)(2,1)S(1)} %shard_map.76.refs_2_.refs_3_), custom_call_target="tpu_custom_call" | custom-call | flops 339738624 | bytes 1404928 | tf_op jit(solution)/shard_map/pallas_call | solution.py:39
  12.8 0.0 collective-permute-done.3.refs_4_
  12.8 0.3 collective-permute-done.refs_0_
  13.1 0.8 %shard_map.78 = (f32[16,2304]{1,0:T(8,128)S(1)}, f32[8,128]{1,0:T(8,128)S(1)}) custom-call(bf16[4,9216]{1,0:T(4,128)(2,1)S(1)} %collective-permute-done.refs_0_, bf16[4,9216]{1,0:T(4,128)(2,1)S(1)} %collective-permute-done.1.refs_1_, bf16[2304,256]{1,0:T(8,128)(2,1)S(1)} %shard_map.76.refs_2_.refs_3_, f32[16,32]{1,0:T(8,128)S(1)} %convert_select_fusion.refs_3_, ...), custom_call_target="tpu_custom_call" | custom-call | flops 339738624 | bytes 1560576 | tf_op jit(solution)/shard_map/pallas_call | solution.py:39
  14.0 0.0 collective-permute-start.6
  14.0 1.2 %collective-permute-done.6.refs_2_ = f32[8,128]{1,0:T(8,128)S(1)} collective-permute-done((f32[8,128]{1,0:T(8,128)S(1)}, f32[8,128]{1,0:T(8,128)S(1)}, u32[]{:S(2)}, u32[]{:S(2)}) %collective-permute-start.6) | collective-permute-done | bytes 4128 | tf_op jit(solution)/shard_map/ppermute | solution.py:33
  15.1 1.0 %shard_map.79 = (bf16[152,256]{1,0:T(8,128)(2,1)S(1)}, bf16[152,256]{1,0:T(8,128)(2,1)S(1)}, bf16[152,256]{1,0:T(8,128)(2,1)S(1)}, bf16[152,256]{1,0:T(8,128)(2,...) custom-call(f32[16,2304]{1,0:T(8,128)S(1)} %get-tuple-element.21.refs_0_, f32[8,128]{1,0:T(8,128)S(1)} %get-tuple-element.22.refs_1_, ...), custom_call_target="tpu_custom_call" | custom-call | flops 679477248 | bytes 1802368 | tf_op jit(solution)/shard_map/pallas_call | solution.py:39
  16.1 2.2 %collective-permute-start.10 = (bf16[152,256]{1,0:T(8,128)(2,1)S(1)}, bf16[152,256]{1,0:T(8,128)(2,1)S(1)}, u32[]{:S(2)}, u32[]{:S(2)}) collective-permute-start(bf16[152,256]{1,0:T(8,128)(2,1)S(1)} %get-tuple-element.27), channel_id=1, source_target_pairs={{0,4},{1,5},{2,6},{3,7},{4,0},{5,1},{6,2},{7,3},{8,15},{9,14},{10,... | collective-permute-start | bytes 233480 | tf_op jit(solution)/shard_map/ppermute | solution.py:33
  18.4 0.9 %collective-permute-start.7 = (bf16[152,256]{1,0:T(8,128)(2,1)S(1)}, bf16[152,256]{1,0:T(8,128)(2,1)S(1)}, u32[]{:S(2)}, u32[]{:S(2)}) collective-permute-start(bf16[152,256]{1,0:T(8,128)(2,1)S(1)} %get-tuple-element.24), channel_id=1, source_target_pairs={{0,5},{1,4},{2,7},{3,6},{4,1},{5,0},{6,3},{7,2},{8,11},{9,10},{10,... | collective-permute-start | bytes 233480 | tf_op jit(solution)/shard_map/ppermute | solution.py:33
  19.3 3.0 %collective-permute-start.8 = (bf16[152,256]{1,0:T(8,128)(2,1)S(1)}, bf16[152,256]{1,0:T(8,128)(2,1)S(1)}, u32[]{:S(2)}, u32[]{:S(2)}) collective-permute-start(bf16[152,256]{1,0:T(8,128)(2,1)S(1)} %get-tuple-element.25), channel_id=1, source_target_pairs={{0,6},{1,7},{2,4},{3,5},{4,2},{5,3},{6,0},{7,1},{8,10},{9,11},{10,... | collective-permute-start | bytes 233480 | tf_op jit(solution)/shard_map/ppermute | solution.py:33
  22.2 0.7 %collective-permute-start.9 = (bf16[152,256]{1,0:T(8,128)(2,1)S(1)}, bf16[152,256]{1,0:T(8,128)(2,1)S(1)}, u32[]{:S(2)}, u32[]{:S(2)}) collective-permute-start(bf16[152,256]{1,0:T(8,128)(2,1)S(1)} %get-tuple-element.26), channel_id=1, source_target_pairs={{8,9},{9,8},{10,11},{11,10},{12,13},{13,12},{14,15},{15,14},{24,25... | collective-permute-start | bytes 233480 | tf_op jit(solution)/shard_map/ppermute | solution.py:33
  22.9 0.5 %collective-permute-done.10.refs_4_ = bf16[152,256]{1,0:T(8,128)(2,1)S(1)} collective-permute-done((bf16[152,256]{1,0:T(8,128)(2,1)S(1)}, bf16[152,256]{1,0:T(8,128)(2,1)S(1)}, u32[]{:S(2)}, u32[]{:S(2)}) %collective-permute-start.10) | collective-permute-done | bytes 77856 | tf_op jit(solution)/shard_map/ppermute | solution.py:33
  23.4 1.2 %collective-permute-done.7.refs_1_ = bf16[152,256]{1,0:T(8,128)(2,1)S(1)} collective-permute-done((bf16[152,256]{1,0:T(8,128)(2,1)S(1)}, bf16[152,256]{1,0:T(8,128)(2,1)S(1)}, u32[]{:S(2)}, u32[]{:S(2)}) %collective-permute-start.7) | collective-permute-done | bytes 77856 | tf_op jit(solution)/shard_map/ppermute | solution.py:33
  24.6 1.7 %collective-permute-done.8.refs_2_ = bf16[152,256]{1,0:T(8,128)(2,1)S(1)} collective-permute-done((bf16[152,256]{1,0:T(8,128)(2,1)S(1)}, bf16[152,256]{1,0:T(8,128)(2,1)S(1)}, u32[]{:S(2)}, u32[]{:S(2)}) %collective-permute-start.8) | collective-permute-done | bytes 77856 | tf_op jit(solution)/shard_map/ppermute | solution.py:33
  26.3 0.0 collective-permute-done.9.refs_3_
  26.3 0.1 shard_map.80
  26.4 0.4 %collective-permute-start.11 = (f32[2,40,256]{2,1,0:T(8,128)S(1)}, f32[2,40,256]{2,1,0:T(8,128)S(1)}, u32[]{:S(2)}, u32[]{:S(2)}) collective-permute-start(f32[2,40,256]{2,1,0:T(8,128)S(1)} %get-tuple-element.29), channel_id=1, source_target_pairs={{0,8},{1,9},{2,10},{3,11},{4,12},{5,13},{6,14},{7,15},{8,0},{9,1},... | collective-permute-start | bytes 245768 | tf_op jit(solution)/shard_map/ppermute | solution.py:33
  26.8 0.9 %collective-permute-done.11.given = f32[2,40,256]{2,1,0:T(8,128)S(1)} collective-permute-done((f32[2,40,256]{2,1,0:T(8,128)S(1)}, f32[2,40,256]{2,1,0:T(8,128)S(1)}, u32[]{:S(2)}, u32[]{:S(2)}) %collective-permute-start.11) | collective-permute-done | bytes 81952 | tf_op jit(solution)/shard_map/ppermute | solution.py:33
  27.7 1.6 %collective-permute-start.12 = (f32[40,256]{1,0:T(8,128)S(1)}, f32[40,256]{1,0:T(8,128)S(1)}, u32[]{:S(2)}, u32[]{:S(2)}) collective-permute-start(f32[40,256]{1,0:T(8,128)S(1)} %get-tuple-element.31), channel_id=1, source_target_pairs={{0,16},{1,17},{2,18},{3,19},{4,20},{5,21},{6,22},{7,23},{8,24},{9,... | collective-permute-start | bytes 122888 | tf_op jit(solution)/shard_map/ppermute | solution.py:33
  29.3 2.5 %collective-permute-done.12.refs_1_ = f32[40,256]{1,0:T(8,128)S(1)} collective-permute-done((f32[40,256]{1,0:T(8,128)S(1)}, f32[40,256]{1,0:T(8,128)S(1)}, u32[]{:S(2)}, u32[]{:S(2)}) %collective-permute-start.12) | collective-permute-done | bytes 40992 | tf_op jit(solution)/shard_map/ppermute | solution.py:33
  31.8 0.6 %shard_map.82 = (f32[4,2304]{1,0:T(4,128)}, f32[1,4]{1,0:T(1,128)}) custom-call(f32[40,256]{1,0:T(8,128)S(1)} %get-tuple-element.30.refs_0_, f32[40,256]{1,0:T(8,128)S(1)} %collective-permute-done.12.refs_1_), custom_call_target="tpu_custom_call" | custom-call | flops 1000000 | bytes 118800 | tf_op jit(solution)/shard_map/pallas_call | solution.py:39
  (5 shorter events, 0.0 us)
Async XLA Ops:
  0.6 9.8 %collective-permute-start.2 = (bf16[32,9216]{1,0:T(8,128)(2,1)}, bf16[32,9216]{1,0:T(8,128)(2,1)S(1)}, u32[]{:S(2)}, u32[]{:S(2)}) collective-permute-start(bf16[32,9216]{1,0:T(8,128)(2,1)} %own.1), channel_id=1, source_target_pairs={{0,8},{1,9},{2,10},{3,11},{4,12},{5,13},{6,14},{7,15},{8,0},{9,1},... | collective-permute-start | bytes 1769480 | tf_op jit(solution)/shard_map/ppermute | solution.py:33
  1.1 11.0 %collective-permute-start.4 = (bf16[4,9216]{1,0:T(4,128)(2,1)}, bf16[4,9216]{1,0:T(4,128)(2,1)S(1)}, u32[]{:S(2)}, u32[]{:S(2)}) collective-permute-start(bf16[4,9216]{1,0:T(4,128)(2,1)} %param.6), channel_id=1, source_target_pairs={{0,4},{1,5},{2,6},{3,7},{4,0},{5,1},{6,2},{7,3},{8,15},{9,14},{10,... | collective-permute-start | bytes 221192 | tf_op jit(solution)/shard_map/ppermute | solution.py:33
  4.8 7.4 %collective-permute-start.5 = (bf16[4,9216]{1,0:T(4,128)(2,1)}, bf16[4,9216]{1,0:T(4,128)(2,1)S(1)}, u32[]{:S(2)}, u32[]{:S(2)}) collective-permute-start(bf16[4,9216]{1,0:T(4,128)(2,1)} %param.6), channel_id=1, source_target_pairs={{0,5},{1,4},{2,7},{3,6},{4,1},{5,0},{6,3},{7,2},{8,11},{9,10},{10,... | collective-permute-start | bytes 221192 | tf_op jit(solution)/shard_map/ppermute | solution.py:33
  6.1 7.0 %collective-permute-start = (bf16[4,9216]{1,0:T(4,128)(2,1)}, bf16[4,9216]{1,0:T(4,128)(2,1)S(1)}, u32[]{:S(2)}, u32[]{:S(2)}) collective-permute-start(bf16[4,9216]{1,0:T(4,128)(2,1)} %param.6), channel_id=1, source_target_pairs={{0,6},{1,7},{2,4},{3,5},{4,2},{5,3},{6,0},{7,1},{8,10},{9,11},{10,... | collective-permute-start | bytes 221192 | tf_op jit(solution)/shard_map/ppermute | solution.py:33
  9.7 3.4 %collective-permute-start.1 = (bf16[4,9216]{1,0:T(4,128)(2,1)}, bf16[4,9216]{1,0:T(4,128)(2,1)S(1)}, u32[]{:S(2)}, u32[]{:S(2)}) collective-permute-start(bf16[4,9216]{1,0:T(4,128)(2,1)} %param.6), channel_id=1, source_target_pairs={{0,9},{1,8},{2,11},{3,10},{4,13},{5,12},{6,15},{7,14},{8,0},{9,1},... | collective-permute-start | bytes 221192 | tf_op jit(solution)/shard_map/ppermute | solution.py:33
  10.5 2.4 %collective-permute-start.3 = (f32[16,32]{1,0:T(8,128)S(1)}, f32[16,32]{1,0:T(8,128)S(1)}, u32[]{:S(2)}, u32[]{:S(2)}) collective-permute-start(f32[16,32]{1,0:T(8,128)S(1)} %convert_select_fusion.refs_3_), channel_id=1, source_target_pairs={{0,8},{1,9},{2,10},{3,11},{4,12},{5,13},{6,14},{7,15},{8,0},{9,1},... | collective-permute-start | bytes 6152 | tf_op jit(solution)/shard_map/ppermute | solution.py:33
  11.0 1.1 %copy-start = (bf16[32,9216]{1,0:T(8,128)(2,1)S(1)}, bf16[32,9216]{1,0:T(8,128)(2,1)}, u32[]{:S(2)}) copy-start(bf16[32,9216]{1,0:T(8,128)(2,1)} %own.1) | copy-start | bytes 1769476
  14.0 1.2 %collective-permute-start.6 = (f32[8,128]{1,0:T(8,128)S(1)}, f32[8,128]{1,0:T(8,128)S(1)}, u32[]{:S(2)}, u32[]{:S(2)}) collective-permute-start(f32[8,128]{1,0:T(8,128)S(1)} %get-tuple-element.22.refs_1_), channel_id=1, source_target_pairs={{0,8},{1,9},{2,10},{3,11},{4,12},{5,13},{6,14},{7,15},{8,0},{9,1},... | collective-permute-start | bytes 12296 | tf_op jit(solution)/shard_map/ppermute | solution.py:33
  16.1 7.3 %collective-permute-start.10 = (bf16[152,256]{1,0:T(8,128)(2,1)S(1)}, bf16[152,256]{1,0:T(8,128)(2,1)S(1)}, u32[]{:S(2)}, u32[]{:S(2)}) collective-permute-start(bf16[152,256]{1,0:T(8,128)(2,1)S(1)} %get-tuple-element.27), channel_id=1, source_target_pairs={{0,4},{1,5},{2,6},{3,7},{4,0},{5,1},{6,2},{7,3},{8,15},{9,14},{10,... | collective-permute-start | bytes 233480 | tf_op jit(solution)/shard_map/ppermute | solution.py:33
  18.4 6.2 %collective-permute-start.7 = (bf16[152,256]{1,0:T(8,128)(2,1)S(1)}, bf16[152,256]{1,0:T(8,128)(2,1)S(1)}, u32[]{:S(2)}, u32[]{:S(2)}) collective-permute-start(bf16[152,256]{1,0:T(8,128)(2,1)S(1)} %get-tuple-element.24), channel_id=1, source_target_pairs={{0,5},{1,4},{2,7},{3,6},{4,1},{5,0},{6,3},{7,2},{8,11},{9,10},{10,... | collective-permute-start | bytes 233480 | tf_op jit(solution)/shard_map/ppermute | solution.py:33
  19.3 7.0 %collective-permute-start.8 = (bf16[152,256]{1,0:T(8,128)(2,1)S(1)}, bf16[152,256]{1,0:T(8,128)(2,1)S(1)}, u32[]{:S(2)}, u32[]{:S(2)}) collective-permute-start(bf16[152,256]{1,0:T(8,128)(2,1)S(1)} %get-tuple-element.25), channel_id=1, source_target_pairs={{0,6},{1,7},{2,4},{3,5},{4,2},{5,3},{6,0},{7,1},{8,10},{9,11},{10,... | collective-permute-start | bytes 233480 | tf_op jit(solution)/shard_map/ppermute | solution.py:33
  22.2 4.1 %collective-permute-start.9 = (bf16[152,256]{1,0:T(8,128)(2,1)S(1)}, bf16[152,256]{1,0:T(8,128)(2,1)S(1)}, u32[]{:S(2)}, u32[]{:S(2)}) collective-permute-start(bf16[152,256]{1,0:T(8,128)(2,1)S(1)} %get-tuple-element.26), channel_id=1, source_target_pairs={{8,9},{9,8},{10,11},{11,10},{12,13},{13,12},{14,15},{15,14},{24,25... | collective-permute-start | bytes 233480 | tf_op jit(solution)/shard_map/ppermute | solution.py:33
  26.4 1.3 %collective-permute-start.11 = (f32[2,40,256]{2,1,0:T(8,128)S(1)}, f32[2,40,256]{2,1,0:T(8,128)S(1)}, u32[]{:S(2)}, u32[]{:S(2)}) collective-permute-start(f32[2,40,256]{2,1,0:T(8,128)S(1)} %get-tuple-element.29), channel_id=1, source_target_pairs={{0,8},{1,9},{2,10},{3,11},{4,12},{5,13},{6,14},{7,15},{8,0},{9,1},... | collective-permute-start | bytes 245768 | tf_op jit(solution)/shard_map/ppermute | solution.py:33
  27.7 4.1 %collective-permute-start.12 = (f32[40,256]{1,0:T(8,128)S(1)}, f32[40,256]{1,0:T(8,128)S(1)}, u32[]{:S(2)}, u32[]{:S(2)}) collective-permute-start(f32[40,256]{1,0:T(8,128)S(1)} %get-tuple-element.31), channel_id=1, source_target_pairs={{0,16},{1,17},{2,18},{3,19},{4,20},{5,21},{6,22},{7,23},{8,24},{9,... | collective-permute-start | bytes 122888 | tf_op jit(solution)/shard_map/ppermute | solution.py:33

commit v4 on v3

--- a/solution.py
+++ b/solution.py
@@ -19,7 +19,8 @@
     first = list(range(half, blk - 1)) + [0]
     second = [blk - 1] + list(range(half - 1, 0, -1))
     pairs = list(zip(first, second))
-    order = list(range(1, half)) + [0]
+    order = list(zip(range(half), [0, *range(2, half), 1]))
+    order = order[1:] + order[:1]
     return pairs, order
 
 
@@ -145,8 +146,9 @@
     stats[...] = jnp.concatenate([peak, mass, jnp.zeros((6, LANES), F32)], axis=0)
 
 
-def backward_kernel(pairs, *refs):
+def backward_kernel(pairs, order, *refs):
     taken = range(len(pairs))
+    core = lax.axis_index("dom") & 1
     exps, mine, theirs, stacked = refs[:4]
     sends, (own, evidence, left) = refs[4:-3], refs[-3:]
     total = stacked.shape[0]
@@ -175,9 +177,10 @@
             left[n * rows + 16 * u : n * rows + 16 * (u + 1), :] = rotated
     result = jnp.dot(left[...], stacked[...], preferred_element_type=F32)
     lane = lax.broadcasted_iota(jnp.int32, (extra_rows, step), 1)
-    for n, t in enumerate(taken):
-        piece = jnp.concatenate([weights[n], jnp.zeros((extra_rows - width, 1), F32)], axis=0)
-        block = result[n * rows : (n + 1) * rows, :]
+    blocks = []
+    for t in taken:
+        piece = jnp.concatenate([weights[t], jnp.zeros((extra_rows - width, 1), F32)], axis=0)
+        block = result[t * rows : (t + 1) * rows, :]
         high = piece.astype(BF16).astype(F32)
         middle = (piece - high).astype(BF16).astype(F32)
         low = piece - high - middle
@@ -185,16 +188,17 @@
             own[:rows, :] = block
             own[rows:, :] = jnp.where(lane == 0, piece, 0.0)
         tail = jnp.where(lane == 0, high, jnp.where(lane == 1, middle, jnp.where(lane == 2, low, 0.0)))
-        sends[n][...] = jnp.concatenate([block, tail], axis=0).astype(BF16)
+        blocks.append(jnp.concatenate([block, tail], axis=0))
+    for send, (i, j) in zip(sends, order):
+        send[...] = (blocks[i] if i == j else jnp.where(core == 0, blocks[i], blocks[j])).astype(BF16)
 
 
 def gather_kernel(pairs, width, *refs):
     turns = len(pairs)
-    own, recv, (keep, give) = refs[0], refs[1 : 1 + turns], refs[1 + turns :]
-    core = lax.axis_index("dom") & 1
+    own, recv, outs, split = refs[0], refs[1 : 1 + turns], refs[1 + turns : -1], refs[-1]
+    me = lax.axis_index("dom")
+    core = me & 1
     rows = ROTS * width
-    sides = keep.shape[0]
-    part = rows // (2 * sides)
     value = None
     for t in range(turns):
         block = recv[t][...].astype(F32)
@@ -203,19 +207,12 @@
         value = block if value is None else value + block
     weight = jnp.sum(value[rows : rows + width, :], axis=1, keepdims=True)
     weight = jnp.broadcast_to(weight, (width, value.shape[1]))
-    for s in range(sides):
-        one = value[2 * s * part : (2 * s + 1) * part, :]
-        two = value[(2 * s + 1) * part : (2 * s + 2) * part, :]
-        keep[s, :, :] = jnp.concatenate([jnp.where(core == 0, one, two), weight], axis=0)
-        give[s, :, :] = jnp.concatenate([jnp.where(core == 0, two, one), weight], axis=0)
-
-
-def pair_kernel(keep, given, *refs):
-    outs, both = refs[:-1], refs[-1]
-    side = lax.axis_index("dom") >> 1
-    both[...] = keep[...] + given[...]
-    for s, out in enumerate(outs):
-        out[...] = both[side ^ s]
+    shards = len(outs)
+    part = rows // shards
+    for s in range(shards):
+        split[s, :, :] = jnp.concatenate([value[s * part : (s + 1) * part, :], weight], axis=0)
+    for s in range(shards):
+        outs[s][...] = split[me ^ s]
 
 
 def finish_kernel(width, *refs):
@@ -292,26 +289,22 @@
     stats_other = over_dom(stats, 1)
     message = shape((rows + 8, step), BF16)
     *sends, own, evidence = call(
-        functools.partial(backward_kernel, pairs),
+        functools.partial(backward_kernel, pairs, order),
         [message] * turns + [shape((rows + 8, step), F32), shape((1, count), F32)],
         [exps, stats, stats_other, stacked],
         [pltpu.VMEM((turns * rows, total), BF16)],
         flops=2 * turns * rows * step * total,
     )
-    recv = [over_blk(sends[t], pairs[t]) for t in order]
-    sides, part = dom // 2, rows // dom + width
-    keep, give = call(
-        functools.partial(gather_kernel, [pairs[t] for t in order], width),
-        [shape((sides, part, step), F32)] * 2,
+    ways = [(pairs[i][0], pairs[j][1]) for i, j in order]
+    recv = [over_blk(send, way) for send, way in zip(sends, ways)]
+    part = rows // dom + width
+    parts = call(
+        functools.partial(gather_kernel, ways, width),
+        [shape((part, step), F32)] * dom,
         [own, *recv],
-    )
-    parts = call(
-        pair_kernel,
-        [shape((part, step), F32)] * sides,
-        [keep, over_dom(give, 1)],
-        [pltpu.VMEM((sides, part, step), F32)],
-    )
-    parts = [parts[0]] + [over_dom(parts[s], 2 * s) for s in range(1, sides)]
+        [pltpu.VMEM((dom, part, step), F32)],
+    )
+    parts = [parts[0]] + [over_dom(parts[s], s) for s in [*range(2, dom), 1]]
     sums, weights = call(
         functools.partial(finish_kernel, width),
         [shape((width, pixels // dom), F32), shape((1, width), F32)],

time: 32.6 us -> 32.3 us (level)
  the two profiles are of different devices: /device:TPU:0 before, /device:TPU:1 now
where the time goes in v4:
time: 32.3 us; the launch traced here: 32.1 us
  starting transfers between devices  19.1 us (59%)
  waiting for transfers between devices  7.1 us (22%)
  Pallas kernels  3.32 us (10%)
  local copies, waits for them, and re-layouts  1.06 us (3%)
  other arithmetic  0.78 us (2%)
  between operations  0.73 us (2%)
    ppermute x14, starting transfers between devices, routed(): return lax.ppermute(block, ('dom', 'blk'), pairs)  19.1 us
    ppermute x14, waiting for transfers between devices, routed(): return lax.ppermute(block, ('dom', 'blk'), pairs)  7.1 us
    pallas_call x6, Pallas kernels, call(): pl.pallas_call(kernel, out_shape=tuple(outs), in_specs=[near] * len(args)...  3.32 us
    unnamed x2, local copies, waits for them, and re-layouts  1.06 us
    select_n x1, other arithmetic, body(): lists = jnp.where(row < slots, named, inv_noise[None, :])  0.78 us
  transfers between devices with their start and end apart: 14, of which 6 were waited for; matrix products, arithmetic and copies ran while one was open for 2% of the time, Pallas kernels for 2%

profile of v4, /device:TPU:1, one launch (start us, length us, event | category | flops | bytes accessed | tf_op | source)
XLA Modules:
  0.0 32.1 jit_solution(11266075914955974125)
XLA Ops:
  0.6 0.1 collective-permute-start.2
  0.8 5.7 %collective-permute-start.4 = (bf16[4,9216]{1,0:T(4,128)(2,1)}, bf16[4,9216]{1,0:T(4,128)(2,1)S(1)}, u32[]{:S(2)}, u32[]{:S(2)}) collective-permute-start(bf16[4,9216]{1,0:T(4,128)(2,1)} %param.6), channel_id=1, source_target_pairs={{0,4},{1,5},{2,6},{3,7},{4,0},{5,1},{6,2},{7,3},{8,15},{9,14},{10,... | collective-permute-start | bytes 221192 | tf_op jit(solution)/shard_map/ppermute | solution.py:34
  6.4 0.0 collective-permute-start.5
  6.5 1.4 %collective-permute-start = (bf16[4,9216]{1,0:T(4,128)(2,1)}, bf16[4,9216]{1,0:T(4,128)(2,1)S(1)}, u32[]{:S(2)}, u32[]{:S(2)}) collective-permute-start(bf16[4,9216]{1,0:T(4,128)(2,1)} %param.6), channel_id=1, source_target_pairs={{0,6},{1,7},{2,4},{3,5},{4,2},{5,3},{6,0},{7,1},{8,10},{9,11},{10,... | collective-permute-start | bytes 221192 | tf_op jit(solution)/shard_map/ppermute | solution.py:34
  7.9 1.8 %collective-permute-start.1 = (bf16[4,9216]{1,0:T(4,128)(2,1)}, bf16[4,9216]{1,0:T(4,128)(2,1)S(1)}, u32[]{:S(2)}, u32[]{:S(2)}) collective-permute-start(bf16[4,9216]{1,0:T(4,128)(2,1)} %param.6), channel_id=1, source_target_pairs={{0,9},{1,8},{2,11},{3,10},{4,13},{5,12},{6,15},{7,14},{8,0},{9,1},... | collective-permute-start | bytes 221192 | tf_op jit(solution)/shard_map/ppermute | solution.py:34
  9.7 0.8 %convert_select_fusion.refs_3_ = f32[16,32]{1,0:T(8,128)S(1)} fusion(s32[8,32]{1,0:T(8,128)} %bitcast.3, f32[32]{0:T(128)} %param.7, s32[32]{0:T(128)} %param.9, pred[16]{0:T(512)(128)(4,1)S(1)} %iota_compare_fusion.1), kind=kLoop, calls=%fused_computation | loop fusion | flops 2048 | bytes 3344 | tf_op jit(solution)/shard_map/jit(_where)/select_n | solution.py:265
  10.5 0.0 collective-permute-start.3
  10.6 0.0 copy-start
  10.6 1.1 %copy-done = bf16[32,9216]{1,0:T(8,128)(2,1)S(1)} copy-done((bf16[32,9216]{1,0:T(8,128)(2,1)S(1)}, bf16[32,9216]{1,0:T(8,128)(2,1)}, u32[]{:S(2)}) %copy-start) | copy-done | bytes 589848
  11.6 0.1 shard_map.76.refs_2_.refs_3_
  11.7 0.0 collective-permute-done.5.refs_1_
  11.7 0.6 %shard_map.77 = (f32[8,2304]{1,0:T(8,128)S(1)}, f32[8,128]{1,0:T(8,128)S(1)}) custom-call(bf16[4,9216]{1,0:T(4,128)(2,1)S(1)} %collective-permute-done.4.refs_0_, bf16[4,9216]{1,0:T(4,128)(2,1)S(1)} %collective-permute-done.5.refs_1_, bf16[2304,256]{1,0:T(8,128)(2,1)S(1)} %shard_map.76.refs_2_.refs_3_), custom_call_target="tpu_custom_call" | custom-call | flops 339738624 | bytes 1404928 | tf_op jit(solution)/shard_map/pallas_call | solution.py:40
  12.4 0.0 collective-permute-done.refs_0_
  12.4 0.2 collective-permute-done.1.refs_1_
  12.6 0.8 %shard_map.78 = (f32[16,2304]{1,0:T(8,128)S(1)}, f32[8,128]{1,0:T(8,128)S(1)}) custom-call(bf16[4,9216]{1,0:T(4,128)(2,1)S(1)} %collective-permute-done.refs_0_, bf16[4,9216]{1,0:T(4,128)(2,1)S(1)} %collective-permute-done.1.refs_1_, bf16[2304,256]{1,0:T(8,128)(2,1)S(1)} %shard_map.76.refs_2_.refs_3_, f32[16,32]{1,0:T(8,128)S(1)} %convert_select_fusion.refs_3_, ...), custom_call_target="tpu_custom_call" | custom-call | flops 339738624 | bytes 1560576 | tf_op jit(solution)/shard_map/pallas_call | solution.py:40
  13.4 0.6 %collective-permute-start.6 = (f32[8,128]{1,0:T(8,128)S(1)}, f32[8,128]{1,0:T(8,128)S(1)}, u32[]{:S(2)}, u32[]{:S(2)}) collective-permute-start(f32[8,128]{1,0:T(8,128)S(1)} %get-tuple-element.22.refs_1_), channel_id=1, source_target_pairs={{0,8},{1,9},{2,10},{3,11},{4,12},{5,13},{6,14},{7,15},{8,0},{9,1},... | collective-permute-start | bytes 12296 | tf_op jit(solution)/shard_map/ppermute | solution.py:34
  14.0 0.8 %collective-permute-done.6.refs_2_ = f32[8,128]{1,0:T(8,128)S(1)} collective-permute-done((f32[8,128]{1,0:T(8,128)S(1)}, f32[8,128]{1,0:T(8,128)S(1)}, u32[]{:S(2)}, u32[]{:S(2)}) %collective-permute-start.6) | collective-permute-done | bytes 4128 | tf_op jit(solution)/shard_map/ppermute | solution.py:34
  14.8 1.0 %shard_map.79 = (bf16[152,256]{1,0:T(8,128)(2,1)S(1)}, bf16[152,256]{1,0:T(8,128)(2,1)S(1)}, bf16[152,256]{1,0:T(8,128)(2,1)S(1)}, bf16[152,256]{1,0:T(8,128)(2,...) custom-call(f32[16,2304]{1,0:T(8,128)S(1)} %get-tuple-element.21.refs_0_, f32[8,128]{1,0:T(8,128)S(1)} %get-tuple-element.22.refs_1_, ...), custom_call_target="tpu_custom_call" | custom-call | flops 679477248 | bytes 1802368 | tf_op jit(solution)/shard_map/pallas_call | solution.py:40
  15.8 2.9 %collective-permute-start.10 = (bf16[152,256]{1,0:T(8,128)(2,1)S(1)}, bf16[152,256]{1,0:T(8,128)(2,1)S(1)}, u32[]{:S(2)}, u32[]{:S(2)}) collective-permute-start(bf16[152,256]{1,0:T(8,128)(2,1)S(1)} %get-tuple-element.27), channel_id=1, source_target_pairs={{0,4},{1,5},{2,6},{3,7},{4,0},{5,1},{6,2},{7,3},{8,15},{9,14},{10,... | collective-permute-start | bytes 233480 | tf_op jit(solution)/shard_map/ppermute | solution.py:34
  18.7 0.0 collective-permute-start.7
  18.8 1.1 %collective-permute-start.8 = (bf16[152,256]{1,0:T(8,128)(2,1)S(1)}, bf16[152,256]{1,0:T(8,128)(2,1)S(1)}, u32[]{:S(2)}, u32[]{:S(2)}) collective-permute-start(bf16[152,256]{1,0:T(8,128)(2,1)S(1)} %get-tuple-element.25), channel_id=1, source_target_pairs={{0,6},{1,7},{2,4},{3,5},{4,2},{5,3},{6,0},{7,1},{8,9},{9,8},{10,11... | collective-permute-start | bytes 233480 | tf_op jit(solution)/shard_map/ppermute | solution.py:34
  19.9 3.4 %collective-permute-start.9 = (bf16[152,256]{1,0:T(8,128)(2,1)S(1)}, bf16[152,256]{1,0:T(8,128)(2,1)S(1)}, u32[]{:S(2)}, u32[]{:S(2)}) collective-permute-start(bf16[152,256]{1,0:T(8,128)(2,1)S(1)} %get-tuple-element.26), channel_id=1, source_target_pairs={{8,11},{9,10},{10,9},{11,8},{12,15},{13,14},{14,13},{15,12},{24,27... | collective-permute-start | bytes 233480 | tf_op jit(solution)/shard_map/ppermute | solution.py:34
  23.3 0.0 collective-permute-done.10.refs_4_
  23.3 0.3 collective-permute-done.7.refs_1_
  23.6 3.0 %collective-permute-done.9.refs_3_ = bf16[152,256]{1,0:T(8,128)(2,1)S(1)} collective-permute-done((bf16[152,256]{1,0:T(8,128)(2,1)S(1)}, bf16[152,256]{1,0:T(8,128)(2,1)S(1)}, u32[]{:S(2)}, u32[]{:S(2)}) %collective-permute-start.9) | collective-permute-done | bytes 77856 | tf_op jit(solution)/shard_map/ppermute | solution.py:34
  26.6 0.1 shard_map.80
  26.7 1.3 %collective-permute-start.11 = (f32[40,256]{1,0:T(8,128)S(1)}, f32[40,256]{1,0:T(8,128)S(1)}, u32[]{:S(2)}, u32[]{:S(2)}) collective-permute-start(f32[40,256]{1,0:T(8,128)S(1)} %get-tuple-element.29), channel_id=1, source_target_pairs={{0,16},{1,17},{2,18},{3,19},{4,20},{5,21},{6,22},{7,23},{8,24},{9,... | collective-permute-start | bytes 122888 | tf_op jit(solution)/shard_map/ppermute | solution.py:34
  28.0 0.0 collective-permute-start.12
  28.0 0.6 %collective-permute-start.13 = (f32[40,256]{1,0:T(8,128)S(1)}, f32[40,256]{1,0:T(8,128)S(1)}, u32[]{:S(2)}, u32[]{:S(2)}) collective-permute-start(f32[40,256]{1,0:T(8,128)S(1)} %get-tuple-element.31), channel_id=1, source_target_pairs={{0,8},{1,9},{2,10},{3,11},{4,12},{5,13},{6,14},{7,15},{8,0},{9,1},... | collective-permute-start | bytes 122888 | tf_op jit(solution)/shard_map/ppermute | solution.py:34
  28.6 1.0 %collective-permute-done.11.refs_1_ = f32[40,256]{1,0:T(8,128)S(1)} collective-permute-done((f32[40,256]{1,0:T(8,128)S(1)}, f32[40,256]{1,0:T(8,128)S(1)}, u32[]{:S(2)}, u32[]{:S(2)}) %collective-permute-start.11) | collective-permute-done | bytes 40992 | tf_op jit(solution)/shard_map/ppermute | solution.py:34
  29.6 1.8 %collective-permute-done.12.refs_2_ = f32[40,256]{1,0:T(8,128)S(1)} collective-permute-done((f32[40,256]{1,0:T(8,128)S(1)}, f32[40,256]{1,0:T(8,128)S(1)}, u32[]{:S(2)}, u32[]{:S(2)}) %collective-permute-start.12) | collective-permute-done | bytes 40992 | tf_op jit(solution)/shard_map/ppermute | solution.py:34
  31.4 0.6 %shard_map.81 = (f32[4,2304]{1,0:T(4,128)}, f32[1,4]{1,0:T(1,128)}) custom-call(f32[40,256]{1,0:T(8,128)S(1)} %get-tuple-element.28.refs_0_, f32[40,256]{1,0:T(8,128)S(1)} %collective-permute-done.11.refs_1_, f32[40,256]{1,0:T(8,128)S(1)} %collective-permute-done.12.refs_2_, f32[40,256]{1,0:T(8,128)S(1)} %collective-permute-done.13.refs_3_), custom_call_target="tpu_custom_call" | custom-call | flops 1000000 | bytes 200720 | tf_op jit(solution)/shard_map/pallas_call | solution.py:40
  (6 shorter events, 0.0 us)
Async XLA Ops:
  0.6 9.9 %collective-permute-start.2 = (bf16[32,9216]{1,0:T(8,128)(2,1)}, bf16[32,9216]{1,0:T(8,128)(2,1)S(1)}, u32[]{:S(2)}, u32[]{:S(2)}) collective-permute-start(bf16[32,9216]{1,0:T(8,128)(2,1)} %own.1), channel_id=1, source_target_pairs={{0,8},{1,9},{2,10},{3,11},{4,12},{5,13},{6,14},{7,15},{8,0},{9,1},... | collective-permute-start | bytes 1769480 | tf_op jit(solution)/shard_map/ppermute | solution.py:34
  0.8 11.0 %collective-permute-start.4 = (bf16[4,9216]{1,0:T(4,128)(2,1)}, bf16[4,9216]{1,0:T(4,128)(2,1)S(1)}, u32[]{:S(2)}, u32[]{:S(2)}) collective-permute-start(bf16[4,9216]{1,0:T(4,128)(2,1)} %param.6), channel_id=1, source_target_pairs={{0,4},{1,5},{2,6},{3,7},{4,0},{5,1},{6,2},{7,3},{8,15},{9,14},{10,... | collective-permute-start | bytes 221192 | tf_op jit(solution)/shard_map/ppermute | solution.py:34
  6.4 5.3 %collective-permute-start.5 = (bf16[4,9216]{1,0:T(4,128)(2,1)}, bf16[4,9216]{1,0:T(4,128)(2,1)S(1)}, u32[]{:S(2)}, u32[]{:S(2)}) collective-permute-start(bf16[4,9216]{1,0:T(4,128)(2,1)} %param.6), channel_id=1, source_target_pairs={{0,5},{1,4},{2,7},{3,6},{4,1},{5,0},{6,3},{7,2},{8,11},{9,10},{10,... | collective-permute-start | bytes 221192 | tf_op jit(solution)/shard_map/ppermute | solution.py:34
  6.5 5.9 %collective-permute-start = (bf16[4,9216]{1,0:T(4,128)(2,1)}, bf16[4,9216]{1,0:T(4,128)(2,1)S(1)}, u32[]{:S(2)}, u32[]{:S(2)}) collective-permute-start(bf16[4,9216]{1,0:T(4,128)(2,1)} %param.6), channel_id=1, source_target_pairs={{0,6},{1,7},{2,4},{3,5},{4,2},{5,3},{6,0},{7,1},{8,10},{9,11},{10,... | collective-permute-start | bytes 221192 | tf_op jit(solution)/shard_map/ppermute | solution.py:34
  7.9 4.7 %collective-permute-start.1 = (bf16[4,9216]{1,0:T(4,128)(2,1)}, bf16[4,9216]{1,0:T(4,128)(2,1)S(1)}, u32[]{:S(2)}, u32[]{:S(2)}) collective-permute-start(bf16[4,9216]{1,0:T(4,128)(2,1)} %param.6), channel_id=1, source_target_pairs={{0,9},{1,8},{2,11},{3,10},{4,13},{5,12},{6,15},{7,14},{8,0},{9,1},... | collective-permute-start | bytes 221192 | tf_op jit(solution)/shard_map/ppermute | solution.py:34
  10.5 1.9 %collective-permute-start.3 = (f32[16,32]{1,0:T(8,128)S(1)}, f32[16,32]{1,0:T(8,128)S(1)}, u32[]{:S(2)}, u32[]{:S(2)}) collective-permute-start(f32[16,32]{1,0:T(8,128)S(1)} %convert_select_fusion.refs_3_), channel_id=1, source_target_pairs={{0,8},{1,9},{2,10},{3,11},{4,12},{5,13},{6,14},{7,15},{8,0},{9,1},... | collective-permute-start | bytes 6152 | tf_op jit(solution)/shard_map/ppermute | solution.py:34
  10.6 1.1 %copy-start = (bf16[32,9216]{1,0:T(8,128)(2,1)S(1)}, bf16[32,9216]{1,0:T(8,128)(2,1)}, u32[]{:S(2)}) copy-start(bf16[32,9216]{1,0:T(8,128)(2,1)} %own.1) | copy-start | bytes 1769476
  13.4 1.4 %collective-permute-start.6 = (f32[8,128]{1,0:T(8,128)S(1)}, f32[8,128]{1,0:T(8,128)S(1)}, u32[]{:S(2)}, u32[]{:S(2)}) collective-permute-start(f32[8,128]{1,0:T(8,128)S(1)} %get-tuple-element.22.refs_1_), channel_id=1, source_target_pairs={{0,8},{1,9},{2,10},{3,11},{4,12},{5,13},{6,14},{7,15},{8,0},{9,1},... | collective-permute-start | bytes 12296 | tf_op jit(solution)/shard_map/ppermute | solution.py:34
  15.8 7.4 %collective-permute-start.10 = (bf16[152,256]{1,0:T(8,128)(2,1)S(1)}, bf16[152,256]{1,0:T(8,128)(2,1)S(1)}, u32[]{:S(2)}, u32[]{:S(2)}) collective-permute-start(bf16[152,256]{1,0:T(8,128)(2,1)S(1)} %get-tuple-element.27), channel_id=1, source_target_pairs={{0,4},{1,5},{2,6},{3,7},{4,0},{5,1},{6,2},{7,3},{8,15},{9,14},{10,... | collective-permute-start | bytes 233480 | tf_op jit(solution)/shard_map/ppermute | solution.py:34
  18.7 4.9 %collective-permute-start.7 = (bf16[152,256]{1,0:T(8,128)(2,1)S(1)}, bf16[152,256]{1,0:T(8,128)(2,1)S(1)}, u32[]{:S(2)}, u32[]{:S(2)}) collective-permute-start(bf16[152,256]{1,0:T(8,128)(2,1)S(1)} %get-tuple-element.24), channel_id=1, source_target_pairs={{0,5},{1,4},{2,7},{3,6},{4,1},{5,0},{6,3},{7,2},{8,10},{9,11},{10,... | collective-permute-start | bytes 233480 | tf_op jit(solution)/shard_map/ppermute | solution.py:34
  18.8 4.8 %collective-permute-start.8 = (bf16[152,256]{1,0:T(8,128)(2,1)S(1)}, bf16[152,256]{1,0:T(8,128)(2,1)S(1)}, u32[]{:S(2)}, u32[]{:S(2)}) collective-permute-start(bf16[152,256]{1,0:T(8,128)(2,1)S(1)} %get-tuple-element.25), channel_id=1, source_target_pairs={{0,6},{1,7},{2,4},{3,5},{4,2},{5,3},{6,0},{7,1},{8,9},{9,8},{10,11... | collective-permute-start | bytes 233480 | tf_op jit(solution)/shard_map/ppermute | solution.py:34
  19.9 6.7 %collective-permute-start.9 = (bf16[152,256]{1,0:T(8,128)(2,1)S(1)}, bf16[152,256]{1,0:T(8,128)(2,1)S(1)}, u32[]{:S(2)}, u32[]{:S(2)}) collective-permute-start(bf16[152,256]{1,0:T(8,128)(2,1)S(1)} %get-tuple-element.26), channel_id=1, source_target_pairs={{8,11},{9,10},{10,9},{11,8},{12,15},{13,14},{14,13},{15,12},{24,27... | collective-permute-start | bytes 233480 | tf_op jit(solution)/shard_map/ppermute | solution.py:34
  26.7 2.9 %collective-permute-start.11 = (f32[40,256]{1,0:T(8,128)S(1)}, f32[40,256]{1,0:T(8,128)S(1)}, u32[]{:S(2)}, u32[]{:S(2)}) collective-permute-start(f32[40,256]{1,0:T(8,128)S(1)} %get-tuple-element.29), channel_id=1, source_target_pairs={{0,16},{1,17},{2,18},{3,19},{4,20},{5,21},{6,22},{7,23},{8,24},{9,... | collective-permute-start | bytes 122888 | tf_op jit(solution)/shard_map/ppermute | solution.py:34
  28.0 3.4 %collective-permute-start.12 = (f32[40,256]{1,0:T(8,128)S(1)}, f32[40,256]{1,0:T(8,128)S(1)}, u32[]{:S(2)}, u32[]{:S(2)}) collective-permute-start(f32[40,256]{1,0:T(8,128)S(1)} %get-tuple-element.30), channel_id=1, source_target_pairs={{0,24},{1,25},{2,26},{3,27},{4,28},{5,29},{6,30},{7,31},{8,16},{9,... | collective-permute-start | bytes 122888 | tf_op jit(solution)/shard_map/ppermute | solution.py:34
  28.0 3.4 %collective-permute-start.13 = (f32[40,256]{1,0:T(8,128)S(1)}, f32[40,256]{1,0:T(8,128)S(1)}, u32[]{:S(2)}, u32[]{:S(2)}) collective-permute-start(f32[40,256]{1,0:T(8,128)S(1)} %get-tuple-element.31), channel_id=1, source_target_pairs={{0,8},{1,9},{2,10},{3,11},{4,12},{5,13},{6,14},{7,15},{8,0},{9,1},... | collective-permute-start | bytes 122888 | tf_op jit(solution)/shard_map/ppermute | solution.py:34
